TPU v7x, 256 devices: a whole 4x4x8 slice. The times are simulated.
256 devices in a mesh: facet: 16 (over x, z_hi), freq: 16 (over z_lo, y, core).
Axes of the slice: x: 4, y: 4, z: 8 (z_hi: 4, z_lo: 2; z = z_hi * 2 + z_lo), core: 2. Of those that a mesh axis runs over, the one named last changes fastest.
Arguments:
- facet_image: bfloat16 [16, 2, 512, 4096], P('facet', None, 'freq'), may hold values from -6 to 6
- facet_offsets: int32 [16, 2], replicated, may hold values from 0 to 32767
- subgrid_rows: int32 [32], replicated, may hold values from 0 to 32767
- column_offset: int32 [1], replicated, may hold values from 0 to 32767
- uv_coords: int32 [2, 256, 8, 512], P(None, ('freq', 'facet')), may hold values from 0 to 255
- observed: bfloat16 [2, 256, 8, 512], P(None, ('freq', 'facet')), may hold values from -6 to 6
Outputs:
- image_residual: bfloat16 [16, 2, 512, 4096], P('facet', None, 'freq')
- residual_vis: bfloat16 [2, 256, 8, 512], P(None, ('freq', 'facet'))
All inputs are finite; a program needn't handle non-finite values.
Results may differ from a plain program's by a relative error of at most 0.024.
Values may be sent and summed in bfloat16 or wider, within the bound.
A program may use at most 64 MiB of HBM per device.

v0:
```python
import math

import jax
import jax.numpy as jnp
from jax import lax
from jax.experimental import pallas as pl
from jax.experimental.pallas import tpu as pltpu
from jax.sharding import PartitionSpec as P

IMAGE = 32768
CONTRIB = 128
SUBGRID = 256
PATCH = 32
SIDE = 8
PERIOD = 256
COL_STEP = 8
ROW_STEP = 64
STEP = 128
FACETS = 16
FREQS = 16
ROWS_DEV = 32
FACET_ROWS = FREQS * ROWS_DEV
FACET_W = 4096
SUBGRIDS = 32
OWN = 2
VIS = 512
LANES = 128
BLOCKS = FACET_W // LANES
PAIR = 2 * CONTRIB

TWO_PI = 2.0 * math.pi
MESH = pl.DeviceIdType.MESH
F32 = jnp.float32
BF16 = jnp.bfloat16


def iota(shape, dim):
    return lax.broadcasted_iota(jnp.int32, shape, dim)


def wrap(m):
    return m & (IMAGE - 1)


def cis(m, period=IMAGE):
    quarter = period // 4
    m = m & (period - 1)
    turn = lax.shift_right_logical(m + quarter // 2, int(math.log2(quarter)))
    rest = (m - turn * quarter).astype(F32) * (TWO_PI / period)
    sq = rest * rest
    sin = 1.0 / 120.0 + sq * (-1.0 / 5040.0 + sq * (1.0 / 362880.0))
    sin = rest + rest * (sq * (-1.0 / 6.0 + sq * sin))
    cos = 1.0 / 24.0 + sq * (-1.0 / 720.0 + sq * (1.0 / 40320.0))
    cos = 1.0 + sq * (-0.5 + sq * cos)
    odd = (turn & 1) == 1
    c = jnp.where(odd, sin, cos)
    s = jnp.where(odd, cos, sin)
    c = jnp.where(((turn + 1) & 2) == 2, -c, c)
    s = jnp.where((turn & 2) == 2, -s, s)
    return c, s


def cmul(a, b):
    return a[0] * b[0] - a[1] * b[1], a[0] * b[1] + a[1] * b[0]


def outer(fine, coarse):
    rows = [
        cmul(fine, (coarse[0][h : h + 1], coarse[1][h : h + 1])) for h in range(coarse[0].shape[0])
    ]
    return jnp.concatenate([r[0] for r in rows], 0), jnp.concatenate([r[1] for r in rows], 0)


def dot(a, b):
    return jnp.dot(a, b, preferred_element_type=F32)


def kernel(
    offs_s,
    starts_s,
    col_s,
    offs_v,
    facet_in,
    uv_in,
    seen_in,
    img_out,
    res_out,
    facet_v,
    uv_v,
    seen_v,
    wide,
    prod,
    col_w,
    back_w,
    tw_r,
    tw_i,
    row_t,
    row_h,
    spread_t,
    spread_h,
    grid_w,
    narrow_w,
    ph_r,
    ph_i,
    eu_r,
    eu_i,
    ev,
    quad,
    weigh,
    shifted,
    gath,
    send_b,
    recv_b,
    send_c,
    recv_c,
    send_d,
    recv_d,
    in_sem,
    out_sem,
    tx_sem,
    rx_sem,
):
    f = lax.axis_index("facet")
    q = lax.axis_index("freq")

    load = pltpu.make_async_copy(facet_in, facet_v, in_sem.at[0])
    load.start()
    load_uv = pltpu.make_async_copy(uv_in, uv_v, in_sem.at[1])
    load_uv.start()
    load_seen = pltpu.make_async_copy(seen_in, seen_v, in_sem.at[2])
    load_seen.start()

    barrier = pltpu.get_barrier_semaphore()
    for i in range(1, FACETS):
        pl.semaphore_signal(
            barrier, inc=1, device_id={"facet": lax.rem(f + i, FACETS)}, device_id_type=MESH
        )
    for i in range(1, FREQS):
        pl.semaphore_signal(
            barrier, inc=1, device_id={"freq": lax.rem(q + i, FREQS)}, device_id_type=MESH
        )

    a = offs_s[f, 0]
    b = offs_s[f, 1]
    column = col_s[0]
    start0 = starts_s[OWN * q]
    start1 = starts_s[OWN * q + 1]

    def exchange(stage, axis, me, count, src, dst):
        copies = []
        for i in range(1, count):
            peer = lax.rem(me + i, count)
            copies.append(
                pltpu.make_async_remote_copy(
                    src_ref=src(peer),
                    dst_ref=dst.at[me],
                    send_sem=tx_sem.at[stage, i],
                    recv_sem=rx_sem.at[stage, i],
                    device_id={axis: peer},
                    device_id_type=MESH,
                )
            )
        for copy in copies:
            copy.start()
        return copies

    freq_l = wrap(column + COL_STEP * iota((8, LANES), 1))
    fine = cis(freq_l * iota((8, LANES), 0))
    freq_h = wrap(column + COL_STEP * iota((16, LANES), 1))
    coarse = cis(freq_h * (8 * iota((16, LANES), 0)))
    tr, ti = outer(fine, coarse)
    ti = -ti
    col_w[0:LANES, 0:LANES] = tr.astype(BF16)
    col_w[0:LANES, LANES:] = ti.astype(BF16)
    col_w[LANES:, 0:LANES] = (-ti).astype(BF16)
    col_w[LANES:, LANES:] = tr.astype(BF16)
    freq_b = wrap(column + COL_STEP * iota((BLOCKS, LANES), 1))
    wr, wi = cis(freq_b * wrap(b + LANES * iota((BLOCKS, LANES), 0)))
    tw_r[...] = wr
    tw_i[...] = wi

    load.wait()
    for y in range(BLOCKS):
        rows = slice(ROWS_DEV * y, ROWS_DEV * (y + 1))
        lanes = slice(LANES * y, LANES * (y + 1))
        wide[rows, 0:LANES] = facet_v[0:ROWS_DEV, lanes]
        wide[rows, LANES:] = facet_v[ROWS_DEV:, lanes]
    prod[...] = dot(wide[...], col_w[...])
    acc_r = jnp.zeros((ROWS_DEV, LANES), F32)
    acc_i = jnp.zeros((ROWS_DEV, LANES), F32)
    for y in range(BLOCKS):
        rows = slice(ROWS_DEV * y, ROWS_DEV * (y + 1))
        dr, di = prod[rows, 0:LANES], prod[rows, LANES:]
        cr, ci = tw_r[y : y + 1, :], tw_i[y : y + 1, :]
        acc_r += dr * cr + di * ci
        acc_i += di * cr - dr * ci
    transformed = jnp.concatenate([acc_r, acc_i], 1) * (1.0 / math.sqrt(FACET_W))
    gath[q] = transformed.astype(BF16)

    pl.semaphore_wait(barrier, FACETS - 1 + FREQS - 1)
    copies_a = exchange(0, "freq", q, FREQS, lambda peer: gath.at[q], gath)

    place = wrap(a + iota((8, FACET_ROWS), 1))
    coarse = cis(8 * ROW_STEP * iota((16, FACET_ROWS), 0) * wrap(a + iota((16, FACET_ROWS), 1)))
    for j, start in enumerate((start0, start1)):
        fine = cis(wrap(start + ROW_STEP * iota((8, FACET_ROWS), 0)) * place)
        rr, ri = outer(fine, coarse)
        row_t[CONTRIB * j : CONTRIB * (j + 1), :] = rr.astype(BF16)
        row_t[PAIR + CONTRIB * j : PAIR + CONTRIB * (j + 1), :] = (-ri).astype(BF16)

    lane_k = iota((8, CONTRIB), 1)
    fine = cis(iota((8, CONTRIB), 0) * wrap(STEP * lane_k + a))
    coarse = cis(8 * iota((32, CONTRIB), 0) * wrap(STEP * iota((32, CONTRIB), 1) + a))
    sr, si = outer(fine, coarse)
    spread_t[0:SUBGRID, :] = sr.astype(BF16)
    spread_t[SUBGRID:, :] = si.astype(BF16)

    fine = cis(STEP * iota((8, SUBGRID), 0) * iota((8, SUBGRID), 1))
    coarse = cis(8 * STEP * iota((16, SUBGRID), 0) * iota((16, SUBGRID), 1))
    gr, gi = outer(fine, coarse)
    grid_w[0:CONTRIB, 0:SUBGRID] = gr.astype(BF16)
    grid_w[0:CONTRIB, SUBGRID:] = gi.astype(BF16)
    grid_w[CONTRIB:, 0:SUBGRID] = (-gi).astype(BF16)
    grid_w[CONTRIB:, SUBGRID:] = gr.astype(BF16)

    shift_b = jnp.broadcast_to(offs_v[:, 1:2], (FACETS, SUBGRID))
    pr, pi = cis(iota((FACETS, SUBGRID), 1) * shift_b)
    ph_r[...] = pr
    ph_i[...] = pi

    for copy in copies_a:
        copy.wait_recv()
    rows_all = gath[...].reshape(FACET_ROWS, PAIR)
    both = dot(row_t[...], rows_all)
    cr = both[0:PAIR, 0:CONTRIB] - both[PAIR:, CONTRIB:]
    ci = both[0:PAIR, CONTRIB:] + both[PAIR:, 0:CONTRIB]
    contrib = (jnp.concatenate([cr, ci], 1) * (1.0 / math.sqrt(FACET_ROWS))).astype(BF16)
    for j in range(OWN):
        both = dot(spread_t[...], contrib[CONTRIB * j : CONTRIB * (j + 1), :])
        sr = both[0:SUBGRID, 0:CONTRIB] - both[SUBGRID:, CONTRIB:]
        si = both[0:SUBGRID, CONTRIB:] + both[SUBGRID:, 0:CONTRIB]
        part = jnp.concatenate([sr, si], 1).astype(BF16)
        send_b[SIDE * j : SIDE * (j + 1)] = part.reshape(SIDE, PATCH, PAIR)
    copies_b = exchange(1, "facet", f, FACETS, lambda peer: send_b.at[peer], recv_b)
    recv_b[f] = send_b[f]

    load_uv.wait()
    load_seen.wait()

    def patch_rows(coords):
        cell = iota((8, VIS), 0)
        by8 = cis(8 * coords, PERIOD)
        by16 = cis(16 * coords, PERIOD)
        for c in range(SIDE):
            row = jnp.broadcast_to(coords[c : c + 1], (8, VIS))
            low = cis(cell * row, PERIOD)
            mid = cmul(low, (by8[0][c : c + 1], by8[1][c : c + 1]))
            half = (jnp.concatenate([low[0], mid[0]], 0), jnp.concatenate([low[1], mid[1]], 0))
            high = cmul(half, (by16[0][c : c + 1], by16[1][c : c + 1]))
            yield (
                c,
                jnp.concatenate([half[0], high[0]], 0),
                jnp.concatenate([half[1], high[1]], 0),
            )

    for c, er, ei in patch_rows(uv_v[0:SIDE, :]):
        eu_r[PATCH * c : PATCH * (c + 1), :] = er
        eu_i[PATCH * c : PATCH * (c + 1), :] = ei
    for c, er, ei in patch_rows(uv_v[SIDE:, :]):
        ev[PATCH * c : PATCH * (c + 1), :] = er.astype(BF16)
        ev[SUBGRID + PATCH * c : SUBGRID + PATCH * (c + 1), :] = ei.astype(BF16)

    fine = cis(STEP * iota((8, CONTRIB), 0) * lane_k)
    coarse = cis(8 * STEP * iota((32, CONTRIB), 0) * iota((32, CONTRIB), 1))
    nr, ni = outer(fine, coarse)
    narrow_w[0:SUBGRID, 0:CONTRIB] = nr.astype(BF16)
    narrow_w[0:SUBGRID, CONTRIB:] = (-ni).astype(BF16)
    narrow_w[SUBGRID:, 0:CONTRIB] = ni.astype(BF16)
    narrow_w[SUBGRID:, CONTRIB:] = nr.astype(BF16)

    fine = cis(wrap(STEP * iota((8, SUBGRID), 0) + a) * iota((8, SUBGRID), 1))
    coarse = cis(8 * STEP * iota((16, SUBGRID), 0) * iota((16, SUBGRID), 1))
    hr, hi = outer(fine, coarse)
    spread_h[0:CONTRIB, :] = hr.astype(BF16)
    spread_h[CONTRIB:, :] = (-hi).astype(BF16)

    def own_freq(rows):
        lane = iota((rows, PAIR), 1)
        start = jnp.where(lane < CONTRIB, start0, start1)
        return wrap(start + ROW_STEP * (lane & (CONTRIB - 1)))

    fine = cis(own_freq(8) * wrap(a + iota((8, PAIR), 0)))
    coarse = cis(own_freq(FACET_ROWS // 8) * (8 * iota((FACET_ROWS // 8, PAIR), 0)))
    hr, hi = outer(fine, coarse)
    row_h[0:FACET_ROWS, :] = hr.astype(BF16)
    row_h[FACET_ROWS:, :] = hi.astype(BF16)

    fine = cis(wrap(column + COL_STEP * iota((8, LANES), 0)) * iota((8, LANES), 1))
    coarse = cis(8 * COL_STEP * iota((16, LANES), 0) * iota((16, LANES), 1))
    br, bi = outer(fine, coarse)
    back_w[0:LANES, 0:LANES] = br.astype(BF16)
    back_w[0:LANES, LANES:] = bi.astype(BF16)
    back_w[LANES:, 0:LANES] = (-bi).astype(BF16)
    back_w[LANES:, LANES:] = br.astype(BF16)

    for copy in copies_b:
        copy.wait_recv()
    quad[...] = dot(recv_b[...].reshape(FACETS * PATCH, PAIR), grid_w[...])
    grid_r = jnp.zeros((PATCH, SUBGRID), F32)
    grid_i = jnp.zeros((PATCH, SUBGRID), F32)
    for g in range(FACETS):
        rows = slice(PATCH * g, PATCH * (g + 1))
        qr, qi = quad[rows, 0:SUBGRID], quad[rows, SUBGRID:]
        pr, pi = ph_r[g : g + 1, :], ph_i[g : g + 1, :]
        grid_r += qr * pr - qi * pi
        grid_i += qr * pi + qi * pr
    grid_r = grid_r * (1.0 / CONTRIB)
    grid_i = grid_i * (1.0 / CONTRIB)

    patch_of = lax.shift_right_logical(iota((PATCH, SUBGRID), 1), 5)
    for c in range(SIDE):
        mine = patch_of == c
        gr = jnp.where(mine, grid_r, 0.0)
        gi = jnp.where(mine, grid_i, 0.0)
        rows = slice(PATCH * c, PATCH * (c + 1))
        low = slice(SUBGRID + PATCH * c, SUBGRID + PATCH * (c + 1))
        weigh[rows, 0:SUBGRID] = gr.astype(BF16)
        weigh[rows, SUBGRID:] = (-gi).astype(BF16)
        weigh[low, 0:SUBGRID] = gi.astype(BF16)
        weigh[low, SUBGRID:] = gr.astype(BF16)
    quad[...] = dot(weigh[...], ev[...])
    models_r, models_i = [], []
    for c in range(SIDE):
        rows = slice(PATCH * c, PATCH * (c + 1))
        low = slice(SUBGRID + PATCH * c, SUBGRID + PATCH * (c + 1))
        inner_r, inner_i = quad[rows, :], quad[low, :]
        ur, ui = eu_r[rows, :], eu_i[rows, :]
        models_r.append(jnp.sum(ur * inner_r - ui * inner_i, axis=0, keepdims=True))
        models_i.append(jnp.sum(ur * inner_i + ui * inner_r, axis=0, keepdims=True))
    model = jnp.concatenate(models_r + models_i, 0) * (1.0 / PATCH)
    residual = (seen_v[...].astype(F32) - model).astype(BF16)
    res_out[...] = residual
    residual = residual.astype(F32)
    for c in range(SIDE):
        rows = slice(PATCH * c, PATCH * (c + 1))
        low = slice(SUBGRID + PATCH * c, SUBGRID + PATCH * (c + 1))
        rr, ri = residual[c : c + 1, :], residual[SIDE + c : SIDE + c + 1, :]
        ur, ui = eu_r[rows, :], eu_i[rows, :]
        weigh[rows, :] = (rr * ur + ri * ui).astype(BF16)
        weigh[low, :] = (ri * ur - rr * ui).astype(BF16)
    quad[...] = lax.dot_general(
        weigh[...], ev[...], (((1,), (1,)), ((), ())), preferred_element_type=F32
    )
    back_r = jnp.zeros((PATCH, SUBGRID), F32)
    back_i = jnp.zeros((PATCH, SUBGRID), F32)
    for c in range(SIDE):
        mine = patch_of == c
        rows = slice(PATCH * c, PATCH * (c + 1))
        low = slice(SUBGRID + PATCH * c, SUBGRID + PATCH * (c + 1))
        back_r = jnp.where(mine, quad[rows, 0:SUBGRID] + quad[low, SUBGRID:], back_r)
        back_i = jnp.where(mine, quad[low, 0:SUBGRID] - quad[rows, SUBGRID:], back_i)
    back_r = back_r * (1.0 / math.sqrt(VIS))
    back_i = back_i * (1.0 / math.sqrt(VIS))

    for g in range(FACETS):
        rows = slice(PATCH * g, PATCH * (g + 1))
        pr, pi = ph_r[g : g + 1, :], ph_i[g : g + 1, :]
        shifted[rows, 0:SUBGRID] = (back_r * pr + back_i * pi).astype(BF16)
        shifted[rows, SUBGRID:] = (back_i * pr - back_r * pi).astype(BF16)
    narrowed = dot(shifted[...], narrow_w[...]).astype(BF16)
    send_c[...] = narrowed.reshape(FACETS, PATCH, PAIR)
    copies_c = exchange(2, "facet", f, FACETS, lambda peer: send_c.at[peer], recv_c)
    recv_c[f] = send_c[f]

    for copy in copies_c:
        copy.wait_recv()
    came_back = recv_c[...].reshape(OWN, SUBGRID, PAIR)
    adjoint = []
    for j in range(OWN):
        both = dot(spread_h[...], came_back[j])
        ar = both[0:CONTRIB, 0:CONTRIB] - both[CONTRIB:, CONTRIB:]
        ai = both[0:CONTRIB, CONTRIB:] + both[CONTRIB:, 0:CONTRIB]
        adjoint.append((jnp.concatenate([ar, ai], 1) * (1.0 / SUBGRID)).astype(BF16))
    both = dot(row_h[...], jnp.concatenate(adjoint, 0))
    rr = both[0:FACET_ROWS, 0:CONTRIB] - both[FACET_ROWS:, CONTRIB:]
    ri = both[0:FACET_ROWS, CONTRIB:] + both[FACET_ROWS:, 0:CONTRIB]
    rows_sum = jnp.concatenate([rr, ri], 1).astype(BF16)
    send_d[...] = rows_sum.reshape(FREQS, ROWS_DEV, PAIR)
    copies_d = exchange(3, "freq", q, FREQS, lambda peer: send_d.at[peer], recv_d)
    recv_d[q] = send_d[q]

    for copy in copies_d:
        copy.wait_recv()
    total = jnp.zeros((ROWS_DEV, PAIR), F32)
    for g in range(FREQS):
        total += recv_d[g].astype(F32)
    total = total * (1.0 / (math.sqrt(SUBGRIDS * CONTRIB) * math.sqrt(CONTRIB)))
    tot_r, tot_i = total[:, 0:CONTRIB], total[:, CONTRIB:]
    for y in range(BLOCKS):
        rows = slice(ROWS_DEV * y, ROWS_DEV * (y + 1))
        cr, ci = tw_r[y : y + 1, :], tw_i[y : y + 1, :]
        wide[rows, 0:LANES] = (tot_r * cr - tot_i * ci).astype(BF16)
        wide[rows, LANES:] = (tot_r * ci + tot_i * cr).astype(BF16)
    prod[...] = dot(wide[...], back_w[...])
    for y in range(BLOCKS):
        rows = slice(ROWS_DEV * y, ROWS_DEV * (y + 1))
        lanes = slice(LANES * y, LANES * (y + 1))
        facet_v[0:ROWS_DEV, lanes] = prod[rows, 0:LANES].astype(BF16)
        facet_v[ROWS_DEV:, lanes] = prod[rows, LANES:].astype(BF16)
    store = pltpu.make_async_copy(facet_v, img_out, out_sem.at[0])
    store.start()
    for copies in (copies_a, copies_b, copies_c, copies_d):
        for copy in copies:
            copy.wait_send()
    store.wait()


def on_device(facet_image, facet_offsets, subgrid_rows, column_offset, uv_coords, observed):
    smem = pl.BlockSpec(memory_space=pltpu.SMEM)
    vmem = pl.BlockSpec(memory_space=pltpu.VMEM)
    hbm = pl.BlockSpec(memory_space=pl.ANY)
    chunk = pltpu.VMEM((16, 32, PAIR), BF16)
    image, residual = pl.pallas_call(
        kernel,
        out_shape=(
            jax.ShapeDtypeStruct((2 * ROWS_DEV, FACET_W), BF16),
            jax.ShapeDtypeStruct((2 * SIDE, VIS), BF16),
        ),
        in_specs=[smem, smem, smem, vmem, hbm, hbm, hbm],
        out_specs=(hbm, vmem),
        scratch_shapes=[
            pltpu.VMEM((2 * ROWS_DEV, FACET_W), BF16),
            pltpu.VMEM((2 * SIDE, VIS), jnp.int32),
            pltpu.VMEM((2 * SIDE, VIS), BF16),
            pltpu.VMEM((BLOCKS * ROWS_DEV, PAIR), BF16),
            pltpu.VMEM((BLOCKS * ROWS_DEV, PAIR), F32),
            pltpu.VMEM((PAIR, PAIR), BF16),
            pltpu.VMEM((PAIR, PAIR), BF16),
            pltpu.VMEM((BLOCKS, LANES), F32),
            pltpu.VMEM((BLOCKS, LANES), F32),
            pltpu.VMEM((2 * PAIR, FACET_ROWS), BF16),
            pltpu.VMEM((2 * FACET_ROWS, PAIR), BF16),
            pltpu.VMEM((2 * SUBGRID, CONTRIB), BF16),
            pltpu.VMEM((2 * CONTRIB, SUBGRID), BF16),
            pltpu.VMEM((PAIR, 2 * SUBGRID), BF16),
            pltpu.VMEM((2 * SUBGRID, PAIR), BF16),
            pltpu.VMEM((FACETS, SUBGRID), F32),
            pltpu.VMEM((FACETS, SUBGRID), F32),
            pltpu.VMEM((SUBGRID, VIS), F32),
            pltpu.VMEM((SUBGRID, VIS), F32),
            pltpu.VMEM((2 * SUBGRID, VIS), BF16),
            pltpu.VMEM((2 * SUBGRID, 2 * SUBGRID), F32),
            pltpu.VMEM((2 * SUBGRID, 2 * SUBGRID), BF16),
            pltpu.VMEM((2 * SUBGRID, 2 * SUBGRID), BF16),
            chunk,
            chunk,
            chunk,
            chunk,
            chunk,
            chunk,
            chunk,
            pltpu.SemaphoreType.DMA((3,)),
            pltpu.SemaphoreType.DMA((1,)),
            pltpu.SemaphoreType.DMA((4, 16)),
            pltpu.SemaphoreType.DMA((4, 16)),
        ],
        compiler_params=pltpu.CompilerParams(
            collective_id=0, has_side_effects=True, vmem_limit_bytes=40 * 1024 * 1024
        ),
    )(
        facet_offsets,
        subgrid_rows,
        column_offset,
        facet_offsets,
        facet_image.reshape(2 * ROWS_DEV, FACET_W),
        uv_coords.reshape(2 * SIDE, VIS),
        observed.reshape(2 * SIDE, VIS),
    )
    return (
        image.reshape(1, 2, ROWS_DEV, FACET_W),
        residual.reshape(2, 1, SIDE, VIS),
    )


def solution(mesh):
    return jax.shard_map(
        on_device,
        mesh=mesh,
        in_specs=(
            P("facet", None, "freq", None),
            P(),
            P(),
            P(),
            P(None, ("freq", "facet"), None, None),
            P(None, ("freq", "facet"), None, None),
        ),
        out_specs=(P("facet", None, "freq", None), P(None, ("freq", "facet"), None, None)),
        check_vma=False,
    )
```

profile of v0, /device:TPU:1, one launch (start us, length us, event | category | flops | bytes accessed | tf_op | source)
XLA Modules:
  0.0 50.1 jit_solution(7218858972829181864)
XLA Ops:
  0.6 0.0 copy-start.2
  1.3 0.0 copy-start.3
  1.3 0.8 %copy.8.offs_s.offs_v = s32[16,2]{1,0:T(8,128)S(1)} copy(s32[16,2]{0,1:T(2,128)} %param.7) | data formatting | bytes 256 | tf_op args[1]
  2.1 0.0 copy-done.2
  2.1 0.0 copy-done.3
  2.1 0.0 copy-start
  2.1 1.0 %copy-done = bf16[1,2,32,4096]{3,2,1,0:T(8,128)(2,1)S(1)} copy-done((bf16[1,2,32,4096]{3,2,1,0:T(8,128)(2,1)S(1)}, bf16[1,2,32,4096]{3,2,1,0:T(8,128)(2,1)}, u32[]{:S(2)}) %copy-start) | copy-done | bytes 524312
  3.1 0.0 copy-start.1
  3.1 0.8 %copy-done.1 = s32[2,1,8,512]{3,2,1,0:T(8,128)S(1)} copy-done((s32[2,1,8,512]{3,2,1,0:T(8,128)S(1)}, s32[2,1,8,512]{3,2,1,0:T(8,128)}, u32[]{:S(2)}) %copy-start.1) | copy-done | bytes 32792
  3.9 44.9 %shard_map.77 = (bf16[64,4096]{1,0:T(8,128)(2,1)S(1)}, bf16[16,512]{1,0:T(8,128)(2,1)S(1)}) custom-call(s32[16,2]{1,0:T(8,128)S(1)} %copy.8.offs_s.offs_v, s32[32]{0:T(128)S(1)} %copy-done.3, s32[1]{0:T(128)S(6)} %copy.13.col_s, s32[16,2]{1,0:T(8,128)S(1)} %copy.8.offs_s.offs_v, bf16[64,4096]{1,0:T(8,128)(2,1)S(1)} %bitcast.7, s32[16,512]{1,0:T(8,128)S(1)} %bitcast.9, ...), custom_call_target="tpu_custom_call" | custom-call | tf_op jit(solution)/shard_map/pallas_call | solution.py:423
  48.7 0.8 %copy.14 = bf16[1,2,32,4096]{3,2,1,0:T(8,128)(2,1)} copy(bf16[1,2,32,4096]{3,2,1,0:T(8,128)(2,1)S(1)} %bitcast.8) | data formatting | bytes 1048576
  49.5 0.6 %copy.15 = bf16[2,1,8,512]{3,2,1,0:T(8,128)(2,1)} copy(bf16[2,1,8,512]{3,2,1,0:T(8,128)(2,1)S(1)} %bitcast.11) | data formatting | bytes 32768
Async XLA Ops:
  0.6 1.4 %copy-start.2 = (bf16[2,1,8,512]{3,2,1,0:T(8,128)(2,1)S(1)}, bf16[2,1,8,512]{3,2,1,0:T(8,128)(2,1)}, u32[]{:S(2)}) copy-start(bf16[2,1,8,512]{3,2,1,0:T(8,128)(2,1)} %param.11) | copy-start | bytes 49156
  1.3 0.8 %copy-start.3 = (s32[32]{0:T(128)S(1)}, s32[32]{0:T(128)}, u32[]{:S(2)}) copy-start(s32[32]{0:T(128)} %starts_s.1) | copy-start | bytes 388
  2.1 1.0 %copy-start = (bf16[1,2,32,4096]{3,2,1,0:T(8,128)(2,1)S(1)}, bf16[1,2,32,4096]{3,2,1,0:T(8,128)(2,1)}, u32[]{:S(2)}) copy-start(bf16[1,2,32,4096]{3,2,1,0:T(8,128)(2,1)} %param.6) | copy-start | bytes 1572868
  3.1 0.8 %copy-start.1 = (s32[2,1,8,512]{3,2,1,0:T(8,128)S(1)}, s32[2,1,8,512]{3,2,1,0:T(8,128)}, u32[]{:S(2)}) copy-start(s32[2,1,8,512]{3,2,1,0:T(8,128)} %param.10) | copy-start | bytes 98308
where the time goes:
time: 50.4 us; the launch traced here: 50.1 us
  Pallas kernels  44.9 us (89%)
  local copies, waits for them, and re-layouts  3.97 us (8%)
  between operations  1.32 us (3%)
    pallas_call x1, Pallas kernels, on_device(): pl.pallas_call(kernel, out_shape=(jax.ShapeDtypeStruct((2 * ROWS_DEV, FAC...  44.9 us
    unnamed x11, local copies, waits for them, and re-layouts  3.97 us

commit v1 on v0

--- a/solution.py
+++ b/solution.py
@@ -27,11 +27,35 @@
 LANES = 128
 BLOCKS = FACET_W // LANES
 PAIR = 2 * CONTRIB
+PARTS = 4
 
 TWO_PI = 2.0 * math.pi
 MESH = pl.DeviceIdType.MESH
 F32 = jnp.float32
 BF16 = jnp.bfloat16
+
+
+def ring_hops(step, size):
+    return min(step, size - step)
+
+
+FACET_STEPS = sorted(
+    [(x, z) for x in range(4) for z in range(4) if x or z],
+    key=lambda s: -ring_hops(s[0], 4) - 2 * ring_hops(s[1], 4),
+)
+FREQ_STEPS = sorted(
+    [(z, y, c) for z in range(2) for y in range(4) for c in range(2) if z or y or c],
+    key=lambda s: -s[0] - ring_hops(s[1], 4),
+)
+
+
+def facet_peer(f, step):
+    return lax.rem(f // 4 + step[0], 4) * 4 + lax.rem(lax.rem(f, 4) + step[1], 4)
+
+
+def freq_peer(q, step):
+    z, y, c = q // 8, lax.rem(q // 2, 4), lax.rem(q, 2)
+    return (lax.rem(z + step[0], 2) * 4 + lax.rem(y + step[1], 4)) * 2 + lax.rem(c + step[2], 2)
 
 
 def iota(shape, dim):
@@ -76,24 +100,25 @@
 
 
 def kernel(
-    offs_s,
-    starts_s,
+    offs_in,
+    starts_in,
     col_s,
-    offs_v,
     facet_in,
     uv_in,
     seen_in,
-    img_out,
+    total_out,
+    tw_r,
+    tw_i,
+    back_w,
     res_out,
+    offs_s,
+    starts_s,
     facet_v,
     uv_v,
     seen_v,
     wide,
     prod,
     col_w,
-    back_w,
-    tw_r,
-    tw_i,
     row_t,
     row_h,
     spread_t,
@@ -116,13 +141,20 @@
     send_d,
     recv_d,
     in_sem,
-    out_sem,
     tx_sem,
     rx_sem,
 ):
     f = lax.axis_index("facet")
     q = lax.axis_index("freq")
 
+    loads = [
+        pltpu.make_async_copy(src, dst, in_sem.at[3 + i])
+        for i, (src, dst) in enumerate(
+            ((offs_in, offs_s), (starts_in, starts_s))
+        )
+    ]
+    for copy in loads:
+        copy.start()
     load = pltpu.make_async_copy(facet_in, facet_v, in_sem.at[0])
     load.start()
     load_uv = pltpu.make_async_copy(uv_in, uv_v, in_sem.at[1])
@@ -131,25 +163,24 @@
     load_seen.start()
 
     barrier = pltpu.get_barrier_semaphore()
-    for i in range(1, FACETS):
-        pl.semaphore_signal(
-            barrier, inc=1, device_id={"facet": lax.rem(f + i, FACETS)}, device_id_type=MESH
-        )
-    for i in range(1, FREQS):
-        pl.semaphore_signal(
-            barrier, inc=1, device_id={"freq": lax.rem(q + i, FREQS)}, device_id_type=MESH
-        )
-
-    a = offs_s[f, 0]
-    b = offs_s[f, 1]
+    facet_peers = [facet_peer(f, step) for step in FACET_STEPS]
+    freq_peers = [freq_peer(q, step) for step in FREQ_STEPS]
+    for peer in facet_peers:
+        pl.semaphore_signal(barrier, inc=1, device_id={"facet": peer}, device_id_type=MESH)
+    for peer in freq_peers:
+        pl.semaphore_signal(barrier, inc=1, device_id={"freq": peer}, device_id_type=MESH)
+
+    for copy in loads:
+        copy.wait()
+    a = offs_s[0, f]
+    b = offs_s[1, f]
     column = col_s[0]
     start0 = starts_s[OWN * q]
     start1 = starts_s[OWN * q + 1]
 
-    def exchange(stage, axis, me, count, src, dst):
+    def exchange(stage, axis, me, peers, src, dst):
         copies = []
-        for i in range(1, count):
-            peer = lax.rem(me + i, count)
+        for i, peer in enumerate(peers):
             copies.append(
                 pltpu.make_async_remote_copy(
                     src_ref=src(peer),
@@ -198,7 +229,7 @@
     gath[q] = transformed.astype(BF16)
 
     pl.semaphore_wait(barrier, FACETS - 1 + FREQS - 1)
-    copies_a = exchange(0, "freq", q, FREQS, lambda peer: gath.at[q], gath)
+    copies_a = exchange(0, "freq", q, freq_peers, lambda peer: gath.at[q], gath)
 
     place = wrap(a + iota((8, FACET_ROWS), 1))
     coarse = cis(8 * ROW_STEP * iota((16, FACET_ROWS), 0) * wrap(a + iota((16, FACET_ROWS), 1)))
@@ -223,7 +254,9 @@
     grid_w[CONTRIB:, 0:SUBGRID] = (-gi).astype(BF16)
     grid_w[CONTRIB:, SUBGRID:] = gr.astype(BF16)
 
-    shift_b = jnp.broadcast_to(offs_v[:, 1:2], (FACETS, SUBGRID))
+    shift_b = jnp.concatenate(
+        [jnp.full((1, SUBGRID), offs_s[1, g], jnp.int32) for g in range(FACETS)], 0
+    )
     pr, pi = cis(iota((FACETS, SUBGRID), 1) * shift_b)
     ph_r[...] = pr
     ph_i[...] = pi
@@ -241,7 +274,7 @@
         si = both[0:SUBGRID, CONTRIB:] + both[SUBGRID:, 0:CONTRIB]
         part = jnp.concatenate([sr, si], 1).astype(BF16)
         send_b[SIDE * j : SIDE * (j + 1)] = part.reshape(SIDE, PATCH, PAIR)
-    copies_b = exchange(1, "facet", f, FACETS, lambda peer: send_b.at[peer], recv_b)
+    copies_b = exchange(1, "facet", f, facet_peers, lambda peer: send_b.at[peer], recv_b)
     recv_b[f] = send_b[f]
 
     load_uv.wait()
@@ -369,7 +402,7 @@
         shifted[rows, SUBGRID:] = (back_i * pr - back_r * pi).astype(BF16)
     narrowed = dot(shifted[...], narrow_w[...]).astype(BF16)
     send_c[...] = narrowed.reshape(FACETS, PATCH, PAIR)
-    copies_c = exchange(2, "facet", f, FACETS, lambda peer: send_c.at[peer], recv_c)
+    copies_c = exchange(2, "facet", f, facet_peers, lambda peer: send_c.at[peer], recv_c)
     recv_c[f] = send_c[f]
 
     for copy in copies_c:
@@ -386,7 +419,7 @@
     ri = both[0:FACET_ROWS, CONTRIB:] + both[FACET_ROWS:, 0:CONTRIB]
     rows_sum = jnp.concatenate([rr, ri], 1).astype(BF16)
     send_d[...] = rows_sum.reshape(FREQS, ROWS_DEV, PAIR)
-    copies_d = exchange(3, "freq", q, FREQS, lambda peer: send_d.at[peer], recv_d)
+    copies_d = exchange(3, "freq", q, freq_peers, lambda peer: send_d.at[peer], recv_d)
     recv_d[q] = send_d[q]
 
     for copy in copies_d:
@@ -395,49 +428,67 @@
     for g in range(FREQS):
         total += recv_d[g].astype(F32)
     total = total * (1.0 / (math.sqrt(SUBGRIDS * CONTRIB) * math.sqrt(CONTRIB)))
-    tot_r, tot_i = total[:, 0:CONTRIB], total[:, CONTRIB:]
-    for y in range(BLOCKS):
-        rows = slice(ROWS_DEV * y, ROWS_DEV * (y + 1))
-        cr, ci = tw_r[y : y + 1, :], tw_i[y : y + 1, :]
-        wide[rows, 0:LANES] = (tot_r * cr - tot_i * ci).astype(BF16)
-        wide[rows, LANES:] = (tot_r * ci + tot_i * cr).astype(BF16)
-    prod[...] = dot(wide[...], back_w[...])
-    for y in range(BLOCKS):
-        rows = slice(ROWS_DEV * y, ROWS_DEV * (y + 1))
-        lanes = slice(LANES * y, LANES * (y + 1))
-        facet_v[0:ROWS_DEV, lanes] = prod[rows, 0:LANES].astype(BF16)
-        facet_v[ROWS_DEV:, lanes] = prod[rows, LANES:].astype(BF16)
-    store = pltpu.make_async_copy(facet_v, img_out, out_sem.at[0])
-    store.start()
+    total_out[...] = total
     for copies in (copies_a, copies_b, copies_c, copies_d):
         for copy in copies:
             copy.wait_send()
-    store.wait()
+
+
+def finish(total, tw_r, tw_i, back_w, residual, img_out, res_out, wide, image, out_sem):
+    res_out[...] = residual[...]
+    tot_r, tot_i = total[:, 0:CONTRIB], total[:, CONTRIB:]
+    stores = []
+    for part in range(PARTS):
+        width = BLOCKS // PARTS
+        for y in range(width * part, width * (part + 1)):
+            rows = slice(ROWS_DEV * y, ROWS_DEV * (y + 1))
+            cr, ci = tw_r[y : y + 1, :], tw_i[y : y + 1, :]
+            wide[rows, 0:LANES] = (tot_r * cr - tot_i * ci).astype(BF16)
+            wide[rows, LANES:] = (tot_r * ci + tot_i * cr).astype(BF16)
+        rows = slice(ROWS_DEV * width * part, ROWS_DEV * width * (part + 1))
+        prod = dot(wide[rows, :], back_w[...]).astype(BF16)
+        for k in range(width):
+            lanes = slice(LANES * (width * part + k), LANES * (width * part + k + 1))
+            rows = slice(ROWS_DEV * k, ROWS_DEV * (k + 1))
+            image[0:ROWS_DEV, lanes] = prod[rows, 0:LANES]
+            image[ROWS_DEV:, lanes] = prod[rows, LANES:]
+        lanes = pl.ds(LANES * width * part, LANES * width)
+        store = pltpu.make_async_copy(image.at[:, lanes], img_out.at[:, lanes], out_sem.at[part])
+        store.start()
+        stores.append(store)
+    for store in stores:
+        store.wait()
+
+
+def in_hbm(x):
+    return pltpu.with_memory_space_constraint(x, pltpu.HBM)
 
 
 def on_device(facet_image, facet_offsets, subgrid_rows, column_offset, uv_coords, observed):
+    vmem = pl.BlockSpec(memory_space=pltpu.VMEM)
     smem = pl.BlockSpec(memory_space=pltpu.SMEM)
-    vmem = pl.BlockSpec(memory_space=pltpu.VMEM)
-    hbm = pl.BlockSpec(memory_space=pl.ANY)
+    hbm = pl.BlockSpec(memory_space=pltpu.HBM)
     chunk = pltpu.VMEM((16, 32, PAIR), BF16)
-    image, residual = pl.pallas_call(
+    *middle, residual = pl.pallas_call(
         kernel,
         out_shape=(
-            jax.ShapeDtypeStruct((2 * ROWS_DEV, FACET_W), BF16),
+            jax.ShapeDtypeStruct((ROWS_DEV, PAIR), F32),
+            jax.ShapeDtypeStruct((BLOCKS, LANES), F32),
+            jax.ShapeDtypeStruct((BLOCKS, LANES), F32),
+            jax.ShapeDtypeStruct((PAIR, PAIR), BF16),
             jax.ShapeDtypeStruct((2 * SIDE, VIS), BF16),
         ),
-        in_specs=[smem, smem, smem, vmem, hbm, hbm, hbm],
-        out_specs=(hbm, vmem),
+        in_specs=[hbm, hbm, smem, hbm, hbm, hbm],
+        out_specs=(vmem,) * 5,
         scratch_shapes=[
+            pltpu.SMEM((2, FACETS), jnp.int32),
+            pltpu.SMEM((SUBGRIDS,), jnp.int32),
             pltpu.VMEM((2 * ROWS_DEV, FACET_W), BF16),
             pltpu.VMEM((2 * SIDE, VIS), jnp.int32),
             pltpu.VMEM((2 * SIDE, VIS), BF16),
             pltpu.VMEM((BLOCKS * ROWS_DEV, PAIR), BF16),
             pltpu.VMEM((BLOCKS * ROWS_DEV, PAIR), F32),
             pltpu.VMEM((PAIR, PAIR), BF16),
-            pltpu.VMEM((PAIR, PAIR), BF16),
-            pltpu.VMEM((BLOCKS, LANES), F32),
-            pltpu.VMEM((BLOCKS, LANES), F32),
             pltpu.VMEM((2 * PAIR, FACET_ROWS), BF16),
             pltpu.VMEM((2 * FACET_ROWS, PAIR), BF16),
             pltpu.VMEM((2 * SUBGRID, CONTRIB), BF16),
@@ -459,23 +510,36 @@
             chunk,
             chunk,
             chunk,
-            pltpu.SemaphoreType.DMA((3,)),
-            pltpu.SemaphoreType.DMA((1,)),
-            pltpu.SemaphoreType.DMA((4, 16)),
-            pltpu.SemaphoreType.DMA((4, 16)),
+            pltpu.SemaphoreType.DMA((6,)),
+            pltpu.SemaphoreType.DMA((4, 15)),
+            pltpu.SemaphoreType.DMA((4, 15)),
         ],
         compiler_params=pltpu.CompilerParams(
-            collective_id=0, has_side_effects=True, vmem_limit_bytes=40 * 1024 * 1024
+            collective_id=0, has_side_effects=True, vmem_limit_bytes=24 * 1024 * 1024
         ),
     )(
-        facet_offsets,
-        subgrid_rows,
+        in_hbm(facet_offsets.T),
+        in_hbm(subgrid_rows),
         column_offset,
-        facet_offsets,
-        facet_image.reshape(2 * ROWS_DEV, FACET_W),
-        uv_coords.reshape(2 * SIDE, VIS),
-        observed.reshape(2 * SIDE, VIS),
+        in_hbm(facet_image.reshape(2 * ROWS_DEV, FACET_W)),
+        in_hbm(uv_coords.reshape(2 * SIDE, VIS)),
+        in_hbm(observed.reshape(2 * SIDE, VIS)),
     )
+    image, residual = pl.pallas_call(
+        finish,
+        out_shape=(
+            jax.ShapeDtypeStruct((2 * ROWS_DEV, FACET_W), BF16),
+            jax.ShapeDtypeStruct((2 * SIDE, VIS), BF16),
+        ),
+        in_specs=[vmem] * 5,
+        out_specs=(hbm, vmem),
+        scratch_shapes=[
+            pltpu.VMEM((BLOCKS * ROWS_DEV, PAIR), BF16),
+            pltpu.VMEM((2 * ROWS_DEV, FACET_W), BF16),
+            pltpu.SemaphoreType.DMA((PARTS,)),
+        ],
+        compiler_params=pltpu.CompilerParams(vmem_limit_bytes=24 * 1024 * 1024),
+    )(*middle, residual)
     return (
         image.reshape(1, 2, ROWS_DEV, FACET_W),
         residual.reshape(2, 1, SIDE, VIS),

time: 50.4 us -> 45.3 us (0.90)
  local copies, waits for them, and re-layouts: 3.97 us -> 0 us
  Pallas kernels: 44.9 us -> 43.9 us
    unnamed x11 -> x0, local copies, waits for them, and re-layouts: 3.97 us -> none
    pallas_call x1 -> x2, Pallas kernels: 44.9 us -> 43.9 us  [the longest x1 42.2 us: on_device(): pl.pallas_call(kernel, out_shape=(jax.ShapeDtypeStruct((ROWS_DEV, PAIR),...]
where the time goes in v1:
time: 45.3 us; the launch traced here: 45.2 us
  Pallas kernels  43.9 us (97%)
  between operations  1.28 us (3%)
    pallas_call x1, Pallas kernels, on_device(): pl.pallas_call(kernel, out_shape=(jax.ShapeDtypeStruct((ROWS_DEV, PAIR),...  42.2 us
    pallas_call x1, Pallas kernels, on_device(): pl.pallas_call(finish, out_shape=(jax.ShapeDtypeStruct((2 * ROWS_DEV, FAC...  1.72 us

profile of v1, /device:TPU:1, one launch (start us, length us, event | category | flops | bytes accessed | tf_op | source)
XLA Modules:
  0.0 45.2 jit_solution(2834270835183425968)
XLA Ops:
  1.3 42.2 %shard_map.77 = (f32[32,256]{1,0:T(8,128)S(1)}, f32[32,128]{1,0:T(8,128)S(1)}, f32[32,128]{1,0:T(8,128)S(1)}, bf16[256,256]{1,0:T(8,128)(2,1)S(1)}, bf16[16,512]{1,0:T(8,128)(2,1)S(1)}) custom-call(s32[2,16]{1,0:T(2,128)} %bitcast.11, s32[32]{0:T(128)} %starts_in.1, s32[1]{0:T(128)S(6)} %copy.9.col_s, bf16[64,4096]{1,0:T(8,128)(2,1)} %bitcast.8, ...), custom_call_target="tpu_custom_call" | custom-call | tf_op jit(solution)/shard_map/pallas_call | solution.py:472
  43.5 1.7 %shard_map.78 = (bf16[64,4096]{1,0:T(8,128)(2,1)}, bf16[16,512]{1,0:T(8,128)(2,1)}) custom-call(f32[32,256]{1,0:T(8,128)S(1)} %get-tuple-element.9.total, f32[32,128]{1,0:T(8,128)S(1)} %get-tuple-element.10.tw_r, f32[32,128]{1,0:T(8,128)S(1)} %get-tuple-element.11.tw_i, bf16[256,256]{1,0:T(8,128)(2,1)S(1)} %get-tuple-element.12.back_w, ...), custom_call_target="tpu_custom_call" | custom-call | tf_op jit(solution)/shard_map/pallas_call | solution.py:528

commit v2 on v1

--- a/solution.py
+++ b/solution.py
@@ -28,6 +28,8 @@
 BLOCKS = FACET_W // LANES
 PAIR = 2 * CONTRIB
 PARTS = 4
+HALF = FACET_ROWS // 2
+FAR_Z = (2, 1, 3, 0)
 
 TWO_PI = 2.0 * math.pi
 MESH = pl.DeviceIdType.MESH
@@ -117,7 +119,6 @@
     uv_v,
     seen_v,
     wide,
-    prod,
     col_w,
     row_t,
     row_h,
@@ -131,6 +132,7 @@
     eu_i,
     ev,
     quad,
+    cells,
     weigh,
     shifted,
     gath,
@@ -141,6 +143,7 @@
     send_d,
     recv_d,
     in_sem,
+    load_sem,
     tx_sem,
     rx_sem,
 ):
@@ -155,8 +158,15 @@
     ]
     for copy in loads:
         copy.start()
-    load = pltpu.make_async_copy(facet_in, facet_v, in_sem.at[0])
-    load.start()
+    load = []
+    for i in range(PARTS):
+        lanes = pl.ds(FACET_W // PARTS * i, FACET_W // PARTS)
+        load.append(
+            pltpu.make_async_copy(
+                facet_in.at[:, lanes], facet_v.at[:, lanes], load_sem.at[i]
+            )
+        )
+        load[i].start()
     load_uv = pltpu.make_async_copy(uv_in, uv_v, in_sem.at[1])
     load_uv.start()
     load_seen = pltpu.make_async_copy(seen_in, seen_v, in_sem.at[2])
@@ -178,9 +188,15 @@
     start0 = starts_s[OWN * q]
     start1 = starts_s[OWN * q + 1]
 
+    def facet_group(dz):
+        return [(i, p) for i, p in enumerate(facet_peers) if FACET_STEPS[i][1] == dz]
+
+    def freq_group(dz):
+        return [(i, p) for i, p in enumerate(freq_peers) if FREQ_STEPS[i][0] == dz]
+
     def exchange(stage, axis, me, peers, src, dst):
         copies = []
-        for i, peer in enumerate(peers):
+        for i, peer in peers:
             copies.append(
                 pltpu.make_async_remote_copy(
                     src_ref=src(peer),
@@ -210,41 +226,51 @@
     tw_r[...] = wr
     tw_i[...] = wi
 
-    load.wait()
-    for y in range(BLOCKS):
-        rows = slice(ROWS_DEV * y, ROWS_DEV * (y + 1))
-        lanes = slice(LANES * y, LANES * (y + 1))
-        wide[rows, 0:LANES] = facet_v[0:ROWS_DEV, lanes]
-        wide[rows, LANES:] = facet_v[ROWS_DEV:, lanes]
-    prod[...] = dot(wide[...], col_w[...])
     acc_r = jnp.zeros((ROWS_DEV, LANES), F32)
     acc_i = jnp.zeros((ROWS_DEV, LANES), F32)
-    for y in range(BLOCKS):
-        rows = slice(ROWS_DEV * y, ROWS_DEV * (y + 1))
-        dr, di = prod[rows, 0:LANES], prod[rows, LANES:]
-        cr, ci = tw_r[y : y + 1, :], tw_i[y : y + 1, :]
-        acc_r += dr * cr + di * ci
-        acc_i += di * cr - dr * ci
+    width = BLOCKS // PARTS
+    for part in range(PARTS):
+        load[part].wait()
+        for y in range(width * part, width * (part + 1)):
+            rows = slice(ROWS_DEV * y, ROWS_DEV * (y + 1))
+            lanes = slice(LANES * y, LANES * (y + 1))
+            wide[rows, 0:LANES] = facet_v[0:ROWS_DEV, lanes]
+            wide[rows, LANES:] = facet_v[ROWS_DEV:, lanes]
+        rows = slice(ROWS_DEV * width * part, ROWS_DEV * width * (part + 1))
+        prod = dot(wide[rows, :], col_w[...])
+        for k in range(width):
+            y = width * part + k
+            rows = slice(ROWS_DEV * k, ROWS_DEV * (k + 1))
+            dr, di = prod[rows, 0:LANES], prod[rows, LANES:]
+            cr, ci = tw_r[y : y + 1, :], tw_i[y : y + 1, :]
+            acc_r += dr * cr + di * ci
+            acc_i += di * cr - dr * ci
     transformed = jnp.concatenate([acc_r, acc_i], 1) * (1.0 / math.sqrt(FACET_W))
     gath[q] = transformed.astype(BF16)
 
     pl.semaphore_wait(barrier, FACETS - 1 + FREQS - 1)
-    copies_a = exchange(0, "freq", q, freq_peers, lambda peer: gath.at[q], gath)
+    copies_a = exchange(0, "freq", q, list(enumerate(freq_peers)), lambda peer: gath.at[q], gath)
 
     place = wrap(a + iota((8, FACET_ROWS), 1))
     coarse = cis(8 * ROW_STEP * iota((16, FACET_ROWS), 0) * wrap(a + iota((16, FACET_ROWS), 1)))
     for j, start in enumerate((start0, start1)):
         fine = cis(wrap(start + ROW_STEP * iota((8, FACET_ROWS), 0)) * place)
         rr, ri = outer(fine, coarse)
-        row_t[CONTRIB * j : CONTRIB * (j + 1), :] = rr.astype(BF16)
-        row_t[PAIR + CONTRIB * j : PAIR + CONTRIB * (j + 1), :] = (-ri).astype(BF16)
+        for z in range(2):
+            lanes = slice(HALF * z, HALF * (z + 1))
+            row_t[z, CONTRIB * j : CONTRIB * (j + 1), :] = rr[:, lanes].astype(BF16)
+            low = slice(PAIR + CONTRIB * j, PAIR + CONTRIB * (j + 1))
+            row_t[z, low, :] = (-ri[:, lanes]).astype(BF16)
 
     lane_k = iota((8, CONTRIB), 1)
     fine = cis(iota((8, CONTRIB), 0) * wrap(STEP * lane_k + a))
     coarse = cis(8 * iota((32, CONTRIB), 0) * wrap(STEP * iota((32, CONTRIB), 1) + a))
     sr, si = outer(fine, coarse)
-    spread_t[0:SUBGRID, :] = sr.astype(BF16)
-    spread_t[SUBGRID:, :] = si.astype(BF16)
+    for g in range(SIDE):
+        rows = slice(PATCH * g, PATCH * (g + 1))
+        half = PATCH * (g // 4)
+        spread_t[g % 4, half : half + PATCH, :] = sr[rows].astype(BF16)
+        spread_t[g % 4, 2 * PATCH + half : 3 * PATCH + half, :] = si[rows].astype(BF16)
 
     fine = cis(STEP * iota((8, SUBGRID), 0) * iota((8, SUBGRID), 1))
     coarse = cis(8 * STEP * iota((16, SUBGRID), 0) * iota((16, SUBGRID), 1))
@@ -261,20 +287,33 @@
     ph_r[...] = pr
     ph_i[...] = pi
 
-    for copy in copies_a:
-        copy.wait_recv()
-    rows_all = gath[...].reshape(FACET_ROWS, PAIR)
-    both = dot(row_t[...], rows_all)
+    def own_half(z):
+        return dot(row_t[z], gath[pl.ds(8 * z, 8)].reshape(HALF, PAIR))
+
+    for copy, step in zip(copies_a, FREQ_STEPS):
+        if step[0] == 0:
+            copy.wait_recv()
+    both = own_half(q // 8)
+    for copy, step in zip(copies_a, FREQ_STEPS):
+        if step[0] == 1:
+            copy.wait_recv()
+    both += own_half(1 - q // 8)
     cr = both[0:PAIR, 0:CONTRIB] - both[PAIR:, CONTRIB:]
     ci = both[0:PAIR, CONTRIB:] + both[PAIR:, 0:CONTRIB]
     contrib = (jnp.concatenate([cr, ci], 1) * (1.0 / math.sqrt(FACET_ROWS))).astype(BF16)
-    for j in range(OWN):
-        both = dot(spread_t[...], contrib[CONTRIB * j : CONTRIB * (j + 1), :])
-        sr = both[0:SUBGRID, 0:CONTRIB] - both[SUBGRID:, CONTRIB:]
-        si = both[0:SUBGRID, CONTRIB:] + both[SUBGRID:, 0:CONTRIB]
-        part = jnp.concatenate([sr, si], 1).astype(BF16)
-        send_b[SIDE * j : SIDE * (j + 1)] = part.reshape(SIDE, PATCH, PAIR)
-    copies_b = exchange(1, "facet", f, facet_peers, lambda peer: send_b.at[peer], recv_b)
+    contrib = jnp.concatenate([contrib[CONTRIB * j : CONTRIB * (j + 1)] for j in range(OWN)], 1)
+    copies_b = []
+    for dz in FAR_Z:
+        z = lax.rem(lax.rem(f, 4) + dz, 4)
+        both = dot(spread_t[z], contrib)
+        for j in range(OWN):
+            re, im = slice(PAIR * j, PAIR * j + CONTRIB), slice(PAIR * j + CONTRIB, PAIR * (j + 1))
+            sr = both[0 : 2 * PATCH, re] - both[2 * PATCH :, im]
+            si = both[0 : 2 * PATCH, im] + both[2 * PATCH :, re]
+            part = jnp.concatenate([sr, si], 1).astype(BF16)
+            send_b[8 * j + z] = part[0:PATCH]
+            send_b[8 * j + 4 + z] = part[PATCH:]
+        copies_b += exchange(1, "facet", f, facet_group(dz), lambda peer: send_b.at[peer], recv_b)
     recv_b[f] = send_b[f]
 
     load_uv.wait()
@@ -300,8 +339,9 @@
         eu_r[PATCH * c : PATCH * (c + 1), :] = er
         eu_i[PATCH * c : PATCH * (c + 1), :] = ei
     for c, er, ei in patch_rows(uv_v[SIDE:, :]):
-        ev[PATCH * c : PATCH * (c + 1), :] = er.astype(BF16)
-        ev[SUBGRID + PATCH * c : SUBGRID + PATCH * (c + 1), :] = ei.astype(BF16)
+        first = PATCH * (c % 4)
+        ev[c // 4, first : first + PATCH, :] = er.astype(BF16)
+        ev[c // 4, LANES + first : LANES + first + PATCH, :] = ei.astype(BF16)
 
     fine = cis(STEP * iota((8, CONTRIB), 0) * lane_k)
     coarse = cis(8 * STEP * iota((32, CONTRIB), 0) * iota((32, CONTRIB), 1))
@@ -325,8 +365,10 @@
     fine = cis(own_freq(8) * wrap(a + iota((8, PAIR), 0)))
     coarse = cis(own_freq(FACET_ROWS // 8) * (8 * iota((FACET_ROWS // 8, PAIR), 0)))
     hr, hi = outer(fine, coarse)
-    row_h[0:FACET_ROWS, :] = hr.astype(BF16)
-    row_h[FACET_ROWS:, :] = hi.astype(BF16)
+    for z in range(2):
+        rows = slice(HALF * z, HALF * (z + 1))
+        row_h[z, 0:HALF, :] = hr[rows].astype(BF16)
+        row_h[z, HALF:, :] = hi[rows].astype(BF16)
 
     fine = cis(wrap(column + COL_STEP * iota((8, LANES), 0)) * iota((8, LANES), 1))
     coarse = cis(8 * COL_STEP * iota((16, LANES), 0) * iota((16, LANES), 1))
@@ -336,73 +378,90 @@
     back_w[LANES:, 0:LANES] = (-bi).astype(BF16)
     back_w[LANES:, LANES:] = br.astype(BF16)
 
-    for copy in copies_b:
-        copy.wait_recv()
-    quad[...] = dot(recv_b[...].reshape(FACETS * PATCH, PAIR), grid_w[...])
     grid_r = jnp.zeros((PATCH, SUBGRID), F32)
     grid_i = jnp.zeros((PATCH, SUBGRID), F32)
-    for g in range(FACETS):
-        rows = slice(PATCH * g, PATCH * (g + 1))
-        qr, qi = quad[rows, 0:SUBGRID], quad[rows, SUBGRID:]
-        pr, pi = ph_r[g : g + 1, :], ph_i[g : g + 1, :]
-        grid_r += qr * pr - qi * pi
-        grid_i += qr * pi + qi * pr
+    order_b = [FACET_STEPS[i] for dz in FAR_Z for i, _ in facet_group(dz)]
+    for dz in FAR_Z[::-1]:
+        for copy, step in zip(copies_b, order_b):
+            if step[1] == (4 - dz) % 4:
+                copy.wait_recv()
+        senders = [4 * x + lax.rem(lax.rem(f, 4) + dz, 4) for x in range(4)]
+        rows = jnp.concatenate([recv_b[g] for g in senders], 0)
+        part = dot(rows, grid_w[...])
+        for x, g in enumerate(senders):
+            rows = slice(PATCH * x, PATCH * (x + 1))
+            qr, qi = part[rows, 0:SUBGRID], part[rows, SUBGRID:]
+            pr, pi = ph_r[pl.ds(g, 1), :], ph_i[pl.ds(g, 1), :]
+            grid_r += qr * pr - qi * pi
+            grid_i += qr * pi + qi * pr
     grid_r = grid_r * (1.0 / CONTRIB)
     grid_i = grid_i * (1.0 / CONTRIB)
 
-    patch_of = lax.shift_right_logical(iota((PATCH, SUBGRID), 1), 5)
+    patch_of = lax.shift_right_logical(iota((PATCH, LANES), 1), 5)
     for c in range(SIDE):
-        mine = patch_of == c
-        gr = jnp.where(mine, grid_r, 0.0)
-        gi = jnp.where(mine, grid_i, 0.0)
-        rows = slice(PATCH * c, PATCH * (c + 1))
-        low = slice(SUBGRID + PATCH * c, SUBGRID + PATCH * (c + 1))
-        weigh[rows, 0:SUBGRID] = gr.astype(BF16)
-        weigh[rows, SUBGRID:] = (-gi).astype(BF16)
-        weigh[low, 0:SUBGRID] = gi.astype(BF16)
-        weigh[low, SUBGRID:] = gr.astype(BF16)
-    quad[...] = dot(weigh[...], ev[...])
+        mine = patch_of == c % 4
+        lanes = slice(LANES * (c // 4), LANES * (c // 4 + 1))
+        gr = jnp.where(mine, grid_r[:, lanes], 0.0)
+        gi = jnp.where(mine, grid_i[:, lanes], 0.0)
+        first = PATCH * (c % 4)
+        rows = slice(first, first + PATCH)
+        low = slice(LANES + first, LANES + first + PATCH)
+        cells[c // 4, rows, 0:LANES] = gr.astype(BF16)
+        cells[c // 4, rows, LANES:] = (-gi).astype(BF16)
+        cells[c // 4, low, 0:LANES] = gi.astype(BF16)
+        cells[c // 4, low, LANES:] = gr.astype(BF16)
     models_r, models_i = [], []
+    for h in range(2):
+        quad[h] = dot(cells[h], ev[h])
     for c in range(SIDE):
-        rows = slice(PATCH * c, PATCH * (c + 1))
-        low = slice(SUBGRID + PATCH * c, SUBGRID + PATCH * (c + 1))
-        inner_r, inner_i = quad[rows, :], quad[low, :]
-        ur, ui = eu_r[rows, :], eu_i[rows, :]
+        first = PATCH * (c % 4)
+        inner_r = quad[c // 4, first : first + PATCH, :]
+        inner_i = quad[c // 4, LANES + first : LANES + first + PATCH, :]
+        ur, ui = eu_r[PATCH * c : PATCH * (c + 1), :], eu_i[PATCH * c : PATCH * (c + 1), :]
         models_r.append(jnp.sum(ur * inner_r - ui * inner_i, axis=0, keepdims=True))
         models_i.append(jnp.sum(ur * inner_i + ui * inner_r, axis=0, keepdims=True))
     model = jnp.concatenate(models_r + models_i, 0) * (1.0 / PATCH)
     residual = (seen_v[...].astype(F32) - model).astype(BF16)
     res_out[...] = residual
     residual = residual.astype(F32)
-    for c in range(SIDE):
-        rows = slice(PATCH * c, PATCH * (c + 1))
-        low = slice(SUBGRID + PATCH * c, SUBGRID + PATCH * (c + 1))
-        rr, ri = residual[c : c + 1, :], residual[SIDE + c : SIDE + c + 1, :]
-        ur, ui = eu_r[rows, :], eu_i[rows, :]
-        weigh[rows, :] = (rr * ur + ri * ui).astype(BF16)
-        weigh[low, :] = (ri * ur - rr * ui).astype(BF16)
-    quad[...] = lax.dot_general(
-        weigh[...], ev[...], (((1,), (1,)), ((), ())), preferred_element_type=F32
-    )
-    back_r = jnp.zeros((PATCH, SUBGRID), F32)
-    back_i = jnp.zeros((PATCH, SUBGRID), F32)
-    for c in range(SIDE):
-        mine = patch_of == c
-        rows = slice(PATCH * c, PATCH * (c + 1))
-        low = slice(SUBGRID + PATCH * c, SUBGRID + PATCH * (c + 1))
-        back_r = jnp.where(mine, quad[rows, 0:SUBGRID] + quad[low, SUBGRID:], back_r)
-        back_i = jnp.where(mine, quad[low, 0:SUBGRID] - quad[rows, SUBGRID:], back_i)
+    backs_r, backs_i = [], []
+    for h in range(2):
+        for c in range(4 * h, 4 * (h + 1)):
+            first = PATCH * (c % 4)
+            rr, ri = residual[c : c + 1, :], residual[SIDE + c : SIDE + c + 1, :]
+            ur, ui = eu_r[PATCH * c : PATCH * (c + 1), :], eu_i[PATCH * c : PATCH * (c + 1), :]
+            weigh[h, first : first + PATCH, :] = (rr * ur + ri * ui).astype(BF16)
+            weigh[h, LANES + first : LANES + first + PATCH, :] = (ri * ur - rr * ui).astype(BF16)
+        full = lax.dot_general(
+            weigh[h], ev[h], (((1,), (1,)), ((), ())), preferred_element_type=F32
+        )
+        back_r = jnp.zeros((PATCH, LANES), F32)
+        back_i = jnp.zeros((PATCH, LANES), F32)
+        for c in range(4):
+            mine = patch_of == c
+            rows = slice(PATCH * c, PATCH * (c + 1))
+            low = slice(LANES + PATCH * c, LANES + PATCH * (c + 1))
+            back_r = jnp.where(mine, full[rows, 0:LANES] + full[low, LANES:], back_r)
+            back_i = jnp.where(mine, full[low, 0:LANES] - full[rows, LANES:], back_i)
+        backs_r.append(back_r)
+        backs_i.append(back_i)
+    back_r = jnp.concatenate(backs_r, 1)
+    back_i = jnp.concatenate(backs_i, 1)
     back_r = back_r * (1.0 / math.sqrt(VIS))
     back_i = back_i * (1.0 / math.sqrt(VIS))
 
-    for g in range(FACETS):
-        rows = slice(PATCH * g, PATCH * (g + 1))
-        pr, pi = ph_r[g : g + 1, :], ph_i[g : g + 1, :]
-        shifted[rows, 0:SUBGRID] = (back_r * pr + back_i * pi).astype(BF16)
-        shifted[rows, SUBGRID:] = (back_i * pr - back_r * pi).astype(BF16)
-    narrowed = dot(shifted[...], narrow_w[...]).astype(BF16)
-    send_c[...] = narrowed.reshape(FACETS, PATCH, PAIR)
-    copies_c = exchange(2, "facet", f, facet_peers, lambda peer: send_c.at[peer], recv_c)
+    copies_c = []
+    for n, dz in enumerate(FAR_Z):
+        takers = [4 * x + lax.rem(lax.rem(f, 4) + dz, 4) for x in range(4)]
+        for x, g in enumerate(takers):
+            rows = slice(PATCH * x, PATCH * (x + 1))
+            pr, pi = ph_r[pl.ds(g, 1), :], ph_i[pl.ds(g, 1), :]
+            shifted[n, rows, 0:SUBGRID] = (back_r * pr + back_i * pi).astype(BF16)
+            shifted[n, rows, SUBGRID:] = (back_i * pr - back_r * pi).astype(BF16)
+        narrowed = dot(shifted[n], narrow_w[...]).astype(BF16)
+        for x, g in enumerate(takers):
+            send_c[g] = narrowed[PATCH * x : PATCH * (x + 1)]
+        copies_c += exchange(2, "facet", f, facet_group(dz), lambda peer: send_c.at[peer], recv_c)
     recv_c[f] = send_c[f]
 
     for copy in copies_c:
@@ -414,19 +473,22 @@
         ar = both[0:CONTRIB, 0:CONTRIB] - both[CONTRIB:, CONTRIB:]
         ai = both[0:CONTRIB, CONTRIB:] + both[CONTRIB:, 0:CONTRIB]
         adjoint.append((jnp.concatenate([ar, ai], 1) * (1.0 / SUBGRID)).astype(BF16))
-    both = dot(row_h[...], jnp.concatenate(adjoint, 0))
-    rr = both[0:FACET_ROWS, 0:CONTRIB] - both[FACET_ROWS:, CONTRIB:]
-    ri = both[0:FACET_ROWS, CONTRIB:] + both[FACET_ROWS:, 0:CONTRIB]
-    rows_sum = jnp.concatenate([rr, ri], 1).astype(BF16)
-    send_d[...] = rows_sum.reshape(FREQS, ROWS_DEV, PAIR)
-    copies_d = exchange(3, "freq", q, freq_peers, lambda peer: send_d.at[peer], recv_d)
-    recv_d[q] = send_d[q]
-
-    for copy in copies_d:
+    adjoint = jnp.concatenate(adjoint, 0)
+    copies_d = []
+    for dz in (1, 0):
+        z = lax.rem(q // 8 + dz, 2)
+        both = dot(row_h[z], adjoint)
+        rr = both[0:HALF, 0:CONTRIB] - both[HALF:, CONTRIB:]
+        ri = both[0:HALF, CONTRIB:] + both[HALF:, 0:CONTRIB]
+        rows = jnp.concatenate([rr, ri], 1).astype(BF16)
+        send_d[pl.ds(8 * z, 8)] = rows.reshape(8, ROWS_DEV, PAIR)
+        copies_d += exchange(3, "freq", q, freq_group(dz), lambda peer: send_d.at[peer], recv_d)
+
+    total = send_d[q].astype(F32)
+    order_d = [FREQ_STEPS[i] for dz in (1, 0) for i, _ in freq_group(dz)]
+    for copy, step in list(zip(copies_d, order_d))[::-1]:
         copy.wait_recv()
-    total = jnp.zeros((ROWS_DEV, PAIR), F32)
-    for g in range(FREQS):
-        total += recv_d[g].astype(F32)
+        total += recv_d[freq_peer(q, (-step[0] % 2, -step[1] % 4, -step[2] % 2))].astype(F32)
     total = total * (1.0 / (math.sqrt(SUBGRIDS * CONTRIB) * math.sqrt(CONTRIB)))
     total_out[...] = total
     for copies in (copies_a, copies_b, copies_c, copies_d):
@@ -435,9 +497,9 @@
 
 
 def finish(total, tw_r, tw_i, back_w, residual, img_out, res_out, wide, image, out_sem):
-    res_out[...] = residual[...]
+    stores = [pltpu.make_async_copy(residual, res_out, out_sem.at[PARTS])]
+    stores[0].start()
     tot_r, tot_i = total[:, 0:CONTRIB], total[:, CONTRIB:]
-    stores = []
     for part in range(PARTS):
         width = BLOCKS // PARTS
         for y in range(width * part, width * (part + 1)):
@@ -487,11 +549,10 @@
             pltpu.VMEM((2 * SIDE, VIS), jnp.int32),
             pltpu.VMEM((2 * SIDE, VIS), BF16),
             pltpu.VMEM((BLOCKS * ROWS_DEV, PAIR), BF16),
-            pltpu.VMEM((BLOCKS * ROWS_DEV, PAIR), F32),
             pltpu.VMEM((PAIR, PAIR), BF16),
-            pltpu.VMEM((2 * PAIR, FACET_ROWS), BF16),
-            pltpu.VMEM((2 * FACET_ROWS, PAIR), BF16),
-            pltpu.VMEM((2 * SUBGRID, CONTRIB), BF16),
+            pltpu.VMEM((2, 2 * PAIR, HALF), BF16),
+            pltpu.VMEM((2, 2 * HALF, PAIR), BF16),
+            pltpu.VMEM((4, 4 * PATCH, CONTRIB), BF16),
             pltpu.VMEM((2 * CONTRIB, SUBGRID), BF16),
             pltpu.VMEM((PAIR, 2 * SUBGRID), BF16),
             pltpu.VMEM((2 * SUBGRID, PAIR), BF16),
@@ -499,10 +560,11 @@
             pltpu.VMEM((FACETS, SUBGRID), F32),
             pltpu.VMEM((SUBGRID, VIS), F32),
             pltpu.VMEM((SUBGRID, VIS), F32),
-            pltpu.VMEM((2 * SUBGRID, VIS), BF16),
-            pltpu.VMEM((2 * SUBGRID, 2 * SUBGRID), F32),
-            pltpu.VMEM((2 * SUBGRID, 2 * SUBGRID), BF16),
-            pltpu.VMEM((2 * SUBGRID, 2 * SUBGRID), BF16),
+            pltpu.VMEM((2, SUBGRID, VIS), BF16),
+            pltpu.VMEM((2, SUBGRID, VIS), F32),
+            pltpu.VMEM((2, SUBGRID, SUBGRID), BF16),
+            pltpu.VMEM((2, SUBGRID, VIS), BF16),
+            pltpu.VMEM((4, 4 * PATCH, 2 * SUBGRID), BF16),
             chunk,
             chunk,
             chunk,
@@ -511,6 +573,7 @@
             chunk,
             chunk,
             pltpu.SemaphoreType.DMA((6,)),
+            pltpu.SemaphoreType.DMA((PARTS,)),
             pltpu.SemaphoreType.DMA((4, 15)),
             pltpu.SemaphoreType.DMA((4, 15)),
         ],
@@ -532,11 +595,11 @@
             jax.ShapeDtypeStruct((2 * SIDE, VIS), BF16),
         ),
         in_specs=[vmem] * 5,
-        out_specs=(hbm, vmem),
+        out_specs=(hbm, hbm),
         scratch_shapes=[
             pltpu.VMEM((BLOCKS * ROWS_DEV, PAIR), BF16),
             pltpu.VMEM((2 * ROWS_DEV, FACET_W), BF16),
-            pltpu.SemaphoreType.DMA((PARTS,)),
+            pltpu.SemaphoreType.DMA((PARTS + 1,)),
         ],
         compiler_params=pltpu.CompilerParams(vmem_limit_bytes=24 * 1024 * 1024),
     )(*middle, residual)

time: 45.3 us -> 44.7 us (0.987)
  Pallas kernels: 43.9 us -> 43.3 us
    pallas_call x1, Pallas kernels: 1.72 us -> 1.12 us  [on_device(): pl.pallas_call(finish, out_shape=(jax.ShapeDtypeStruct((2 * ROWS_DEV, FAC...]
where the time goes in v2:
time: 44.7 us; the launch traced here: 44.6 us
  Pallas kernels  43.3 us (97%)
  between operations  1.28 us (3%)
    pallas_call x1, Pallas kernels, on_device(): pl.pallas_call(kernel, out_shape=(jax.ShapeDtypeStruct((ROWS_DEV, PAIR),...  42.2 us
    pallas_call x1, Pallas kernels, on_device(): pl.pallas_call(finish, out_shape=(jax.ShapeDtypeStruct((2 * ROWS_DEV, FAC...  1.12 us

profile of v2, /device:TPU:1, one launch (start us, length us, event | category | flops | bytes accessed | tf_op | source)
XLA Modules:
  0.0 44.6 jit_solution(5669833813182933541)
XLA Ops:
  1.3 42.2 %shard_map.77 = (f32[32,256]{1,0:T(8,128)S(1)}, f32[32,128]{1,0:T(8,128)S(1)}, f32[32,128]{1,0:T(8,128)S(1)}, bf16[256,256]{1,0:T(8,128)(2,1)S(1)}, bf16[16,512]{1,0:T(8,128)(2,1)S(1)}) custom-call(s32[2,16]{1,0:T(2,128)} %bitcast.11, s32[32]{0:T(128)} %starts_in.1, s32[1]{0:T(128)S(6)} %copy.9.col_s, bf16[64,4096]{1,0:T(8,128)(2,1)} %bitcast.8, ...), custom_call_target="tpu_custom_call" | custom-call | tf_op jit(solution)/shard_map/pallas_call | solution.py:534
  43.5 1.1 %shard_map.78 = (bf16[64,4096]{1,0:T(8,128)(2,1)}, bf16[16,512]{1,0:T(8,128)(2,1)}) custom-call(f32[32,256]{1,0:T(8,128)S(1)} %get-tuple-element.9.total, f32[32,128]{1,0:T(8,128)S(1)} %get-tuple-element.10.tw_r, f32[32,128]{1,0:T(8,128)S(1)} %get-tuple-element.11.tw_i, bf16[256,256]{1,0:T(8,128)(2,1)S(1)} %get-tuple-element.12.back_w, ...), custom_call_target="tpu_custom_call" | custom-call | tf_op jit(solution)/shard_map/pallas_call | solution.py:591

commit v3 on v2

--- a/solution.py
+++ b/solution.py
@@ -29,7 +29,6 @@
 PAIR = 2 * CONTRIB
 PARTS = 4
 HALF = FACET_ROWS // 2
-FAR_Z = (2, 1, 3, 0)
 
 TWO_PI = 2.0 * math.pi
 MESH = pl.DeviceIdType.MESH
@@ -41,23 +40,20 @@
     return min(step, size - step)
 
 
-FACET_STEPS = sorted(
-    [(x, z) for x in range(4) for z in range(4) if x or z],
-    key=lambda s: -ring_hops(s[0], 4) - 2 * ring_hops(s[1], 4),
-)
+SPREAD_STEPS = [(x, d) for d in (3, 2, 1, 0) for x in (2, 1, 3, 0) if x or d]
 FREQ_STEPS = sorted(
     [(z, y, c) for z in range(2) for y in range(4) for c in range(2) if z or y or c],
     key=lambda s: -s[0] - ring_hops(s[1], 4),
 )
 
 
-def facet_peer(f, step):
-    return lax.rem(f // 4 + step[0], 4) * 4 + lax.rem(lax.rem(f, 4) + step[1], 4)
-
-
 def freq_peer(q, step):
     z, y, c = q // 8, lax.rem(q // 2, 4), lax.rem(q, 2)
     return (lax.rem(z + step[0], 2) * 4 + lax.rem(y + step[1], 4)) * 2 + lax.rem(c + step[2], 2)
+
+
+def back_step(d):
+    return d if d % 2 else -d
 
 
 def iota(shape, dim):
@@ -173,10 +169,23 @@
     load_seen.start()
 
     barrier = pltpu.get_barrier_semaphore()
-    facet_peers = [facet_peer(f, step) for step in FACET_STEPS]
+    x, chip, other = f // 4, 2 * lax.rem(f, 4) + q // 8, lax.rem(q + 8, FREQS)
+    away = 2 * (q // 8) - 1
+
+    def beside(dx, dz):
+        z = lax.rem(chip + away * dz + 8, 8)
+        return {"facet": 4 * lax.rem(x + dx, 4) + z // 2, "freq": other if dz % 2 else q}
+
+    def target(d):
+        return lax.rem(chip + away * d + 8, 8) // 2
+
+    def origin(d):
+        return lax.rem(chip + away * back_step(d) + 8, 8) // 2
+
     freq_peers = [freq_peer(q, step) for step in FREQ_STEPS]
-    for peer in facet_peers:
-        pl.semaphore_signal(barrier, inc=1, device_id={"facet": peer}, device_id_type=MESH)
+    greeted = [(dx, dz) for dx in range(4) for dz in (0, 1, 2, 3, -2) if dx or dz]
+    for dx, dz in greeted:
+        pl.semaphore_signal(barrier, inc=1, device_id=beside(dx, dz), device_id_type=MESH)
     for peer in freq_peers:
         pl.semaphore_signal(barrier, inc=1, device_id={"freq": peer}, device_id_type=MESH)
 
@@ -185,31 +194,22 @@
     a = offs_s[0, f]
     b = offs_s[1, f]
     column = col_s[0]
-    start0 = starts_s[OWN * q]
-    start1 = starts_s[OWN * q + 1]
-
-    def facet_group(dz):
-        return [(i, p) for i, p in enumerate(facet_peers) if FACET_STEPS[i][1] == dz]
+    starts = [starts_s[OWN * who + j] for who in (q, other) for j in range(OWN)]
 
     def freq_group(dz):
         return [(i, p) for i, p in enumerate(freq_peers) if FREQ_STEPS[i][0] == dz]
 
-    def exchange(stage, axis, me, peers, src, dst):
-        copies = []
-        for i, peer in peers:
-            copies.append(
-                pltpu.make_async_remote_copy(
-                    src_ref=src(peer),
-                    dst_ref=dst.at[me],
-                    send_sem=tx_sem.at[stage, i],
-                    recv_sem=rx_sem.at[stage, i],
-                    device_id={axis: peer},
-                    device_id_type=MESH,
-                )
-            )
-        for copy in copies:
-            copy.start()
-        return copies
+    def send(stage, i, src, dst, device):
+        copy = pltpu.make_async_remote_copy(
+            src_ref=src,
+            dst_ref=dst,
+            send_sem=tx_sem.at[stage, i],
+            recv_sem=rx_sem.at[stage, i],
+            device_id=device,
+            device_id_type=MESH,
+        )
+        copy.start()
+        return copy
 
     freq_l = wrap(column + COL_STEP * iota((8, LANES), 1))
     fine = cis(freq_l * iota((8, LANES), 0))
@@ -248,19 +248,21 @@
     transformed = jnp.concatenate([acc_r, acc_i], 1) * (1.0 / math.sqrt(FACET_W))
     gath[q] = transformed.astype(BF16)
 
-    pl.semaphore_wait(barrier, FACETS - 1 + FREQS - 1)
-    copies_a = exchange(0, "freq", q, list(enumerate(freq_peers)), lambda peer: gath.at[q], gath)
+    pl.semaphore_wait(barrier, len(greeted) + FREQS - 1)
+    copies_a = [
+        send(0, i, gath.at[q], gath.at[q], {"freq": peer}) for i, peer in enumerate(freq_peers)
+    ]
 
     place = wrap(a + iota((8, FACET_ROWS), 1))
     coarse = cis(8 * ROW_STEP * iota((16, FACET_ROWS), 0) * wrap(a + iota((16, FACET_ROWS), 1)))
-    for j, start in enumerate((start0, start1)):
+    for n, start in enumerate(starts):
         fine = cis(wrap(start + ROW_STEP * iota((8, FACET_ROWS), 0)) * place)
         rr, ri = outer(fine, coarse)
+        first = 2 * PAIR * (n // OWN) + CONTRIB * (n % OWN)
         for z in range(2):
             lanes = slice(HALF * z, HALF * (z + 1))
-            row_t[z, CONTRIB * j : CONTRIB * (j + 1), :] = rr[:, lanes].astype(BF16)
-            low = slice(PAIR + CONTRIB * j, PAIR + CONTRIB * (j + 1))
-            row_t[z, low, :] = (-ri[:, lanes]).astype(BF16)
+            row_t[z, first : first + CONTRIB, :] = rr[:, lanes].astype(BF16)
+            row_t[z, PAIR + first : PAIR + first + CONTRIB, :] = (-ri[:, lanes]).astype(BF16)
 
     lane_k = iota((8, CONTRIB), 1)
     fine = cis(iota((8, CONTRIB), 0) * wrap(STEP * lane_k + a))
@@ -298,23 +300,28 @@
         if step[0] == 1:
             copy.wait_recv()
     both += own_half(1 - q // 8)
-    cr = both[0:PAIR, 0:CONTRIB] - both[PAIR:, CONTRIB:]
-    ci = both[0:PAIR, CONTRIB:] + both[PAIR:, 0:CONTRIB]
-    contrib = (jnp.concatenate([cr, ci], 1) * (1.0 / math.sqrt(FACET_ROWS))).astype(BF16)
-    contrib = jnp.concatenate([contrib[CONTRIB * j : CONTRIB * (j + 1)] for j in range(OWN)], 1)
+    contribs = []
+    for e in range(2):
+        top, low = both[2 * PAIR * e : 2 * PAIR * e + PAIR], both[2 * PAIR * e + PAIR : 2 * PAIR * (e + 1)]
+        cr = top[:, 0:CONTRIB] - low[:, CONTRIB:]
+        ci = top[:, CONTRIB:] + low[:, 0:CONTRIB]
+        contrib = (jnp.concatenate([cr, ci], 1) * (1.0 / math.sqrt(FACET_ROWS))).astype(BF16)
+        contribs.append(jnp.concatenate([contrib[0:CONTRIB], contrib[CONTRIB:]], 1))
     copies_b = []
-    for dz in FAR_Z:
-        z = lax.rem(lax.rem(f, 4) + dz, 4)
-        both = dot(spread_t[z], contrib)
+    for d in (3, 2, 1, 0):
+        both = dot(spread_t[target(d)], contribs[d % 2])
         for j in range(OWN):
             re, im = slice(PAIR * j, PAIR * j + CONTRIB), slice(PAIR * j + CONTRIB, PAIR * (j + 1))
             sr = both[0 : 2 * PATCH, re] - both[2 * PATCH :, im]
             si = both[0 : 2 * PATCH, im] + both[2 * PATCH :, re]
             part = jnp.concatenate([sr, si], 1).astype(BF16)
-            send_b[8 * j + z] = part[0:PATCH]
-            send_b[8 * j + 4 + z] = part[PATCH:]
-        copies_b += exchange(1, "facet", f, facet_group(dz), lambda peer: send_b.at[peer], recv_b)
-    recv_b[f] = send_b[f]
+            send_b[4 * d + 2 * j] = part[0:PATCH]
+            send_b[4 * d + 2 * j + 1] = part[PATCH:]
+        for i, step in enumerate(SPREAD_STEPS):
+            if step[1] == d:
+                src = send_b.at[4 * d + lax.rem(x + step[0], 4)]
+                copies_b.append(send(1, i, src, recv_b.at[f], beside(step[0], d)))
+    recv_b[f] = send_b[x]
 
     load_uv.wait()
     load_seen.wait()
@@ -351,19 +358,29 @@
     narrow_w[SUBGRID:, 0:CONTRIB] = ni.astype(BF16)
     narrow_w[SUBGRID:, CONTRIB:] = nr.astype(BF16)
 
-    fine = cis(wrap(STEP * iota((8, SUBGRID), 0) + a) * iota((8, SUBGRID), 1))
-    coarse = cis(8 * STEP * iota((16, SUBGRID), 0) * iota((16, SUBGRID), 1))
-    hr, hi = outer(fine, coarse)
-    spread_h[0:CONTRIB, :] = hr.astype(BF16)
-    spread_h[CONTRIB:, :] = (-hi).astype(BF16)
+    for z in range(4):
+
+        def cell(rows):
+            lane = iota((rows, 2 * PATCH), 1)
+            block = 4 * lax.shift_right_logical(lane, 5) + z
+            return PATCH * block + (lane & (PATCH - 1))
+
+        fine = cis(wrap(STEP * iota((8, 2 * PATCH), 0) + a) * cell(8))
+        coarse = cis(8 * STEP * iota((16, 2 * PATCH), 0) * cell(16))
+        hr, hi = outer(fine, coarse)
+        spread_h[z, 0:CONTRIB, :] = hr.astype(BF16)
+        spread_h[z, CONTRIB:, :] = (-hi).astype(BF16)
 
     def own_freq(rows):
-        lane = iota((rows, PAIR), 1)
-        start = jnp.where(lane < CONTRIB, start0, start1)
+        lane = iota((rows, 2 * PAIR), 1)
+        which = lax.shift_right_logical(lane, 7)
+        start = jnp.where(which == 0, starts[0], starts[1])
+        start = jnp.where(which == 2, starts[2], start)
+        start = jnp.where(which == 3, starts[3], start)
         return wrap(start + ROW_STEP * (lane & (CONTRIB - 1)))
 
-    fine = cis(own_freq(8) * wrap(a + iota((8, PAIR), 0)))
-    coarse = cis(own_freq(FACET_ROWS // 8) * (8 * iota((FACET_ROWS // 8, PAIR), 0)))
+    fine = cis(own_freq(8) * wrap(a + iota((8, 2 * PAIR), 0)))
+    coarse = cis(own_freq(FACET_ROWS // 8) * (8 * iota((FACET_ROWS // 8, 2 * PAIR), 0)))
     hr, hi = outer(fine, coarse)
     for z in range(2):
         rows = slice(HALF * z, HALF * (z + 1))
@@ -380,16 +397,15 @@
 
     grid_r = jnp.zeros((PATCH, SUBGRID), F32)
     grid_i = jnp.zeros((PATCH, SUBGRID), F32)
-    order_b = [FACET_STEPS[i] for dz in FAR_Z for i, _ in facet_group(dz)]
-    for dz in FAR_Z[::-1]:
-        for copy, step in zip(copies_b, order_b):
-            if step[1] == (4 - dz) % 4:
+    for d in range(4):
+        for copy, step in zip(copies_b, SPREAD_STEPS):
+            if step[1] == d:
                 copy.wait_recv()
-        senders = [4 * x + lax.rem(lax.rem(f, 4) + dz, 4) for x in range(4)]
+        senders = [4 * col + origin(d) for col in range(4)]
         rows = jnp.concatenate([recv_b[g] for g in senders], 0)
         part = dot(rows, grid_w[...])
-        for x, g in enumerate(senders):
-            rows = slice(PATCH * x, PATCH * (x + 1))
+        for n, g in enumerate(senders):
+            rows = slice(PATCH * n, PATCH * (n + 1))
             qr, qi = part[rows, 0:SUBGRID], part[rows, SUBGRID:]
             pr, pi = ph_r[pl.ds(g, 1), :], ph_i[pl.ds(g, 1), :]
             grid_r += qr * pr - qi * pi
@@ -451,28 +467,39 @@
     back_i = back_i * (1.0 / math.sqrt(VIS))
 
     copies_c = []
-    for n, dz in enumerate(FAR_Z):
-        takers = [4 * x + lax.rem(lax.rem(f, 4) + dz, 4) for x in range(4)]
-        for x, g in enumerate(takers):
-            rows = slice(PATCH * x, PATCH * (x + 1))
+    for d in (3, 2, 1, 0):
+        for n in range(4):
+            g = 4 * n + origin(d)
+            rows = slice(PATCH * n, PATCH * (n + 1))
             pr, pi = ph_r[pl.ds(g, 1), :], ph_i[pl.ds(g, 1), :]
-            shifted[n, rows, 0:SUBGRID] = (back_r * pr + back_i * pi).astype(BF16)
-            shifted[n, rows, SUBGRID:] = (back_i * pr - back_r * pi).astype(BF16)
-        narrowed = dot(shifted[n], narrow_w[...]).astype(BF16)
-        for x, g in enumerate(takers):
-            send_c[g] = narrowed[PATCH * x : PATCH * (x + 1)]
-        copies_c += exchange(2, "facet", f, facet_group(dz), lambda peer: send_c.at[peer], recv_c)
-    recv_c[f] = send_c[f]
-
-    for copy in copies_c:
-        copy.wait_recv()
-    came_back = recv_c[...].reshape(OWN, SUBGRID, PAIR)
+            shifted[d, rows, 0:SUBGRID] = (back_r * pr + back_i * pi).astype(BF16)
+            shifted[d, rows, SUBGRID:] = (back_i * pr - back_r * pi).astype(BF16)
+        narrowed = dot(shifted[d], narrow_w[...]).astype(BF16)
+        send_c[4 * d : 4 * (d + 1)] = narrowed.reshape(4, PATCH, PAIR)
+        for i, step in enumerate(SPREAD_STEPS):
+            if step[1] == d:
+                src = send_c.at[4 * d + lax.rem(x + step[0], 4)]
+                device = beside(step[0], back_step(d))
+                copies_c.append(send(2, i, src, recv_c.at[4 * d + x], device))
+    recv_c[x] = send_c[x]
+
+    halves = [None, None]
+    for d in range(4):
+        for copy, step in zip(copies_c, SPREAD_STEPS):
+            if step[1] == d:
+                copy.wait_recv()
+        rows = jnp.concatenate(
+            [recv_c[4 * d + 2 * j : 4 * d + 2 * j + 2].reshape(2 * PATCH, PAIR) for j in range(OWN)], 1
+        )
+        part = dot(spread_h[target(d)], rows)
+        halves[d % 2] = part if d < 2 else halves[d % 2] + part
     adjoint = []
-    for j in range(OWN):
-        both = dot(spread_h[...], came_back[j])
-        ar = both[0:CONTRIB, 0:CONTRIB] - both[CONTRIB:, CONTRIB:]
-        ai = both[0:CONTRIB, CONTRIB:] + both[CONTRIB:, 0:CONTRIB]
-        adjoint.append((jnp.concatenate([ar, ai], 1) * (1.0 / SUBGRID)).astype(BF16))
+    for both in halves:
+        for j in range(OWN):
+            re, im = slice(PAIR * j, PAIR * j + CONTRIB), slice(PAIR * j + CONTRIB, PAIR * (j + 1))
+            ar = both[0:CONTRIB, re] - both[CONTRIB:, im]
+            ai = both[0:CONTRIB, im] + both[CONTRIB:, re]
+            adjoint.append((jnp.concatenate([ar, ai], 1) * (1.0 / SUBGRID)).astype(BF16))
     adjoint = jnp.concatenate(adjoint, 0)
     copies_d = []
     for dz in (1, 0):
@@ -482,7 +509,9 @@
         ri = both[0:HALF, CONTRIB:] + both[HALF:, 0:CONTRIB]
         rows = jnp.concatenate([rr, ri], 1).astype(BF16)
         send_d[pl.ds(8 * z, 8)] = rows.reshape(8, ROWS_DEV, PAIR)
-        copies_d += exchange(3, "freq", q, freq_group(dz), lambda peer: send_d.at[peer], recv_d)
+        copies_d += [
+            send(3, i, send_d.at[peer], recv_d.at[q], {"freq": peer}) for i, peer in freq_group(dz)
+        ]
 
     total = send_d[q].astype(F32)
     order_d = [FREQ_STEPS[i] for dz in (1, 0) for i, _ in freq_group(dz)]
@@ -550,10 +579,10 @@
             pltpu.VMEM((2 * SIDE, VIS), BF16),
             pltpu.VMEM((BLOCKS * ROWS_DEV, PAIR), BF16),
             pltpu.VMEM((PAIR, PAIR), BF16),
-            pltpu.VMEM((2, 2 * PAIR, HALF), BF16),
-            pltpu.VMEM((2, 2 * HALF, PAIR), BF16),
+            pltpu.VMEM((2, 4 * PAIR, HALF), BF16),
+            pltpu.VMEM((2, 2 * HALF, 2 * PAIR), BF16),
             pltpu.VMEM((4, 4 * PATCH, CONTRIB), BF16),
-            pltpu.VMEM((2 * CONTRIB, SUBGRID), BF16),
+            pltpu.VMEM((4, 2 * CONTRIB, 2 * PATCH), BF16),
             pltpu.VMEM((PAIR, 2 * SUBGRID), BF16),
             pltpu.VMEM((2 * SUBGRID, PAIR), BF16),
             pltpu.VMEM((FACETS, SUBGRID), F32),

time: 44.7 us -> 44.1 us (0.987)
  Pallas kernels: 43.3 us -> 42.7 us
    pallas_call x1, Pallas kernels: 42.2 us -> 41.6 us  [on_device(): pl.pallas_call(kernel, out_shape=(jax.ShapeDtypeStruct((ROWS_DEV, PAIR),...]
where the time goes in v3:
time: 44.1 us; the launch traced here: 44 us
  Pallas kernels  42.7 us (97%)
  between operations  1.28 us (3%)
    pallas_call x1, Pallas kernels, on_device(): pl.pallas_call(kernel, out_shape=(jax.ShapeDtypeStruct((ROWS_DEV, PAIR),...  41.6 us
    pallas_call x1, Pallas kernels, on_device(): pl.pallas_call(finish, out_shape=(jax.ShapeDtypeStruct((2 * ROWS_DEV, FAC...  1.12 us

profile of v3, /device:TPU:1, one launch (start us, length us, event | category | flops | bytes accessed | tf_op | source)
XLA Modules:
  0.0 44.0 jit_solution(5363464664869511076)
XLA Ops:
  1.3 41.6 %shard_map.77 = (f32[32,256]{1,0:T(8,128)S(1)}, f32[32,128]{1,0:T(8,128)S(1)}, f32[32,128]{1,0:T(8,128)S(1)}, bf16[256,256]{1,0:T(8,128)(2,1)S(1)}, bf16[16,512]{1,0:T(8,128)(2,1)S(1)}) custom-call(s32[2,16]{1,0:T(2,128)} %bitcast.11, s32[32]{0:T(128)} %starts_in.1, s32[1]{0:T(128)S(6)} %copy.9.col_s, bf16[64,4096]{1,0:T(8,128)(2,1)} %bitcast.8, ...), custom_call_target="tpu_custom_call" | custom-call | tf_op jit(solution)/shard_map/pallas_call | solution.py:563
  42.9 1.1 %shard_map.78 = (bf16[64,4096]{1,0:T(8,128)(2,1)}, bf16[16,512]{1,0:T(8,128)(2,1)}) custom-call(f32[32,256]{1,0:T(8,128)S(1)} %get-tuple-element.9.total, f32[32,128]{1,0:T(8,128)S(1)} %get-tuple-element.10.tw_r, f32[32,128]{1,0:T(8,128)S(1)} %get-tuple-element.11.tw_i, bf16[256,256]{1,0:T(8,128)(2,1)S(1)} %get-tuple-element.12.back_w, ...), custom_call_target="tpu_custom_call" | custom-call | tf_op jit(solution)/shard_map/pallas_call | solution.py:620

commit v4 on v3

--- a/solution.py
+++ b/solution.py
@@ -40,7 +40,7 @@
     return min(step, size - step)
 
 
-SPREAD_STEPS = [(x, d) for d in (3, 2, 1, 0) for x in (2, 1, 3, 0) if x or d]
+SPREAD_STEPS = [(x, d) for d in (3, 1, 2, 0) for x in (2, 1, 3, 0) if x or d]
 FREQ_STEPS = sorted(
     [(z, y, c) for z in range(2) for y in range(4) for c in range(2) if z or y or c],
     key=lambda s: -s[0] - ring_hops(s[1], 4),
@@ -91,6 +91,13 @@
         cmul(fine, (coarse[0][h : h + 1], coarse[1][h : h + 1])) for h in range(coarse[0].shape[0])
     ]
     return jnp.concatenate([r[0] for r in rows], 0), jnp.concatenate([r[1] for r in rows], 0)
+
+
+def with_turned(t):
+    turned = []
+    for first in range(0, t.shape[1], PAIR):
+        turned += [-t[:, first + CONTRIB : first + PAIR], t[:, first : first + CONTRIB]]
+    return jnp.concatenate([t, jnp.concatenate(turned, 1)], 0)
 
 
 def dot(a, b):
@@ -228,14 +235,15 @@
 
     acc_r = jnp.zeros((ROWS_DEV, LANES), F32)
     acc_i = jnp.zeros((ROWS_DEV, LANES), F32)
-    width = BLOCKS // PARTS
-    for part in range(PARTS):
-        load[part].wait()
-        for y in range(width * part, width * (part + 1)):
-            rows = slice(ROWS_DEV * y, ROWS_DEV * (y + 1))
-            lanes = slice(LANES * y, LANES * (y + 1))
-            wide[rows, 0:LANES] = facet_v[0:ROWS_DEV, lanes]
-            wide[rows, LANES:] = facet_v[ROWS_DEV:, lanes]
+    for y in range(BLOCKS):
+        if y % (BLOCKS // PARTS) == 0:
+            load[y // (BLOCKS // PARTS)].wait()
+        rows = slice(ROWS_DEV * y, ROWS_DEV * (y + 1))
+        lanes = slice(LANES * y, LANES * (y + 1))
+        wide[rows, 0:LANES] = facet_v[0:ROWS_DEV, lanes]
+        wide[rows, LANES:] = facet_v[ROWS_DEV:, lanes]
+    width = BLOCKS // 1
+    for part in range(1):
         rows = slice(ROWS_DEV * width * part, ROWS_DEV * width * (part + 1))
         prod = dot(wide[rows, :], col_w[...])
         for k in range(width):
@@ -258,11 +266,11 @@
     for n, start in enumerate(starts):
         fine = cis(wrap(start + ROW_STEP * iota((8, FACET_ROWS), 0)) * place)
         rr, ri = outer(fine, coarse)
-        first = 2 * PAIR * (n // OWN) + CONTRIB * (n % OWN)
+        rows = slice(CONTRIB * n, CONTRIB * (n + 1))
         for z in range(2):
             lanes = slice(HALF * z, HALF * (z + 1))
-            row_t[z, first : first + CONTRIB, :] = rr[:, lanes].astype(BF16)
-            row_t[z, PAIR + first : PAIR + first + CONTRIB, :] = (-ri[:, lanes]).astype(BF16)
+            row_t[z, rows, 0:HALF] = rr[:, lanes].astype(BF16)
+            row_t[z, rows, HALF:] = (-ri[:, lanes]).astype(BF16)
 
     lane_k = iota((8, CONTRIB), 1)
     fine = cis(iota((8, CONTRIB), 0) * wrap(STEP * lane_k + a))
@@ -271,8 +279,8 @@
     for g in range(SIDE):
         rows = slice(PATCH * g, PATCH * (g + 1))
         half = PATCH * (g // 4)
-        spread_t[g % 4, half : half + PATCH, :] = sr[rows].astype(BF16)
-        spread_t[g % 4, 2 * PATCH + half : 3 * PATCH + half, :] = si[rows].astype(BF16)
+        spread_t[g % 4, half : half + PATCH, 0:CONTRIB] = sr[rows].astype(BF16)
+        spread_t[g % 4, half : half + PATCH, CONTRIB:] = si[rows].astype(BF16)
 
     fine = cis(STEP * iota((8, SUBGRID), 0) * iota((8, SUBGRID), 1))
     coarse = cis(8 * STEP * iota((16, SUBGRID), 0) * iota((16, SUBGRID), 1))
@@ -290,7 +298,7 @@
     ph_i[...] = pi
 
     def own_half(z):
-        return dot(row_t[z], gath[pl.ds(8 * z, 8)].reshape(HALF, PAIR))
+        return dot(row_t[z], with_turned(gath[pl.ds(8 * z, 8)].reshape(HALF, PAIR)))
 
     for copy, step in zip(copies_a, FREQ_STEPS):
         if step[0] == 0:
@@ -300,27 +308,24 @@
         if step[0] == 1:
             copy.wait_recv()
     both += own_half(1 - q // 8)
-    contribs = []
-    for e in range(2):
-        top, low = both[2 * PAIR * e : 2 * PAIR * e + PAIR], both[2 * PAIR * e + PAIR : 2 * PAIR * (e + 1)]
-        cr = top[:, 0:CONTRIB] - low[:, CONTRIB:]
-        ci = top[:, CONTRIB:] + low[:, 0:CONTRIB]
-        contrib = (jnp.concatenate([cr, ci], 1) * (1.0 / math.sqrt(FACET_ROWS))).astype(BF16)
-        contribs.append(jnp.concatenate([contrib[0:CONTRIB], contrib[CONTRIB:]], 1))
+    contrib = (both * (1.0 / math.sqrt(FACET_ROWS))).astype(BF16)
     copies_b = []
-    for d in (3, 2, 1, 0):
-        both = dot(spread_t[target(d)], contribs[d % 2])
-        for j in range(OWN):
-            re, im = slice(PAIR * j, PAIR * j + CONTRIB), slice(PAIR * j + CONTRIB, PAIR * (j + 1))
-            sr = both[0 : 2 * PATCH, re] - both[2 * PATCH :, im]
-            si = both[0 : 2 * PATCH, im] + both[2 * PATCH :, re]
-            part = jnp.concatenate([sr, si], 1).astype(BF16)
-            send_b[4 * d + 2 * j] = part[0:PATCH]
-            send_b[4 * d + 2 * j + 1] = part[PATCH:]
-        for i, step in enumerate(SPREAD_STEPS):
-            if step[1] == d:
-                src = send_b.at[4 * d + lax.rem(x + step[0], 4)]
-                copies_b.append(send(1, i, src, recv_b.at[f], beside(step[0], d)))
+    for pair in ((3, 1), (2, 0)):
+        first = PAIR * (pair[0] % 2)
+        rows = slice(first, first + CONTRIB), slice(first + CONTRIB, first + PAIR)
+        own = with_turned(jnp.concatenate([contrib[r] for r in rows], 1))
+        table = jnp.concatenate([spread_t[target(d)] for d in pair], 0)
+        parts = dot(table, own).astype(BF16)
+        for n, d in enumerate(pair):
+            for j in range(OWN):
+                for half in range(2):
+                    first = PATCH * (2 * n + half)
+                    part = parts[first : first + PATCH, PAIR * j : PAIR * (j + 1)]
+                    send_b[4 * d + 2 * j + half] = part
+            for i, step in enumerate(SPREAD_STEPS):
+                if step[1] == d:
+                    src = send_b.at[4 * d + lax.rem(x + step[0], 4)]
+                    copies_b.append(send(1, i, src, recv_b.at[f], beside(step[0], d)))
     recv_b[f] = send_b[x]
 
     load_uv.wait()
@@ -361,15 +366,15 @@
     for z in range(4):
 
         def cell(rows):
-            lane = iota((rows, 2 * PATCH), 1)
+            lane = iota((rows, 4 * PATCH), 1) & (2 * PATCH - 1)
             block = 4 * lax.shift_right_logical(lane, 5) + z
             return PATCH * block + (lane & (PATCH - 1))
 
-        fine = cis(wrap(STEP * iota((8, 2 * PATCH), 0) + a) * cell(8))
-        coarse = cis(8 * STEP * iota((16, 2 * PATCH), 0) * cell(16))
+        fine = cis(wrap(STEP * iota((8, 4 * PATCH), 0) + a) * cell(8))
+        coarse = cis(8 * STEP * iota((16, 4 * PATCH), 0) * cell(16))
         hr, hi = outer(fine, coarse)
-        spread_h[z, 0:CONTRIB, :] = hr.astype(BF16)
-        spread_h[z, CONTRIB:, :] = (-hi).astype(BF16)
+        real = iota((CONTRIB, 4 * PATCH), 1) < 2 * PATCH
+        spread_h[z] = jnp.where(real, hr, -hi).astype(BF16)
 
     def own_freq(rows):
         lane = iota((rows, 2 * PAIR), 1)
@@ -384,8 +389,8 @@
     hr, hi = outer(fine, coarse)
     for z in range(2):
         rows = slice(HALF * z, HALF * (z + 1))
-        row_h[z, 0:HALF, :] = hr[rows].astype(BF16)
-        row_h[z, HALF:, :] = hi[rows].astype(BF16)
+        row_h[z, :, 0 : 2 * PAIR] = hr[rows].astype(BF16)
+        row_h[z, :, 2 * PAIR :] = hi[rows].astype(BF16)
 
     fine = cis(wrap(column + COL_STEP * iota((8, LANES), 0)) * iota((8, LANES), 1))
     coarse = cis(8 * COL_STEP * iota((16, LANES), 0) * iota((16, LANES), 1))
@@ -467,20 +472,22 @@
     back_i = back_i * (1.0 / math.sqrt(VIS))
 
     copies_c = []
-    for d in (3, 2, 1, 0):
-        for n in range(4):
-            g = 4 * n + origin(d)
-            rows = slice(PATCH * n, PATCH * (n + 1))
-            pr, pi = ph_r[pl.ds(g, 1), :], ph_i[pl.ds(g, 1), :]
-            shifted[d, rows, 0:SUBGRID] = (back_r * pr + back_i * pi).astype(BF16)
-            shifted[d, rows, SUBGRID:] = (back_i * pr - back_r * pi).astype(BF16)
-        narrowed = dot(shifted[d], narrow_w[...]).astype(BF16)
-        send_c[4 * d : 4 * (d + 1)] = narrowed.reshape(4, PATCH, PAIR)
-        for i, step in enumerate(SPREAD_STEPS):
-            if step[1] == d:
-                src = send_c.at[4 * d + lax.rem(x + step[0], 4)]
-                device = beside(step[0], back_step(d))
-                copies_c.append(send(2, i, src, recv_c.at[4 * d + x], device))
+    for h, pair in enumerate(((3, 1), (2, 0))):
+        for m, d in enumerate(pair):
+            for n in range(4):
+                g = 4 * n + origin(d)
+                rows = slice(PATCH * (4 * m + n), PATCH * (4 * m + n + 1))
+                pr, pi = ph_r[pl.ds(g, 1), :], ph_i[pl.ds(g, 1), :]
+                shifted[h, rows, 0:SUBGRID] = (back_r * pr + back_i * pi).astype(BF16)
+                shifted[h, rows, SUBGRID:] = (back_i * pr - back_r * pi).astype(BF16)
+        narrowed = dot(shifted[h], narrow_w[...]).astype(BF16).reshape(8, PATCH, PAIR)
+        for m, d in enumerate(pair):
+            send_c[4 * d : 4 * (d + 1)] = narrowed[4 * m : 4 * (m + 1)]
+            for i, step in enumerate(SPREAD_STEPS):
+                if step[1] == d:
+                    src = send_c.at[4 * d + lax.rem(x + step[0], 4)]
+                    device = beside(step[0], back_step(d))
+                    copies_c.append(send(2, i, src, recv_c.at[4 * d + x], device))
     recv_c[x] = send_c[x]
 
     halves = [None, None]
@@ -491,24 +498,18 @@
         rows = jnp.concatenate(
             [recv_c[4 * d + 2 * j : 4 * d + 2 * j + 2].reshape(2 * PATCH, PAIR) for j in range(OWN)], 1
         )
-        part = dot(spread_h[target(d)], rows)
+        part = dot(spread_h[target(d)], with_turned(rows))
         halves[d % 2] = part if d < 2 else halves[d % 2] + part
     adjoint = []
     for both in halves:
         for j in range(OWN):
-            re, im = slice(PAIR * j, PAIR * j + CONTRIB), slice(PAIR * j + CONTRIB, PAIR * (j + 1))
-            ar = both[0:CONTRIB, re] - both[CONTRIB:, im]
-            ai = both[0:CONTRIB, im] + both[CONTRIB:, re]
-            adjoint.append((jnp.concatenate([ar, ai], 1) * (1.0 / SUBGRID)).astype(BF16))
-    adjoint = jnp.concatenate(adjoint, 0)
+            own = both[:, PAIR * j : PAIR * (j + 1)]
+            adjoint.append((own * (1.0 / SUBGRID)).astype(BF16))
+    adjoint = with_turned(jnp.concatenate(adjoint, 0))
+    rows = dot(row_h[...].reshape(FACET_ROWS, 4 * PAIR), adjoint).astype(BF16)
+    send_d[...] = rows.reshape(FREQS, ROWS_DEV, PAIR)
     copies_d = []
     for dz in (1, 0):
-        z = lax.rem(q // 8 + dz, 2)
-        both = dot(row_h[z], adjoint)
-        rr = both[0:HALF, 0:CONTRIB] - both[HALF:, CONTRIB:]
-        ri = both[0:HALF, CONTRIB:] + both[HALF:, 0:CONTRIB]
-        rows = jnp.concatenate([rr, ri], 1).astype(BF16)
-        send_d[pl.ds(8 * z, 8)] = rows.reshape(8, ROWS_DEV, PAIR)
         copies_d += [
             send(3, i, send_d.at[peer], recv_d.at[q], {"freq": peer}) for i, peer in freq_group(dz)
         ]
@@ -579,10 +580,10 @@
             pltpu.VMEM((2 * SIDE, VIS), BF16),
             pltpu.VMEM((BLOCKS * ROWS_DEV, PAIR), BF16),
             pltpu.VMEM((PAIR, PAIR), BF16),
-            pltpu.VMEM((2, 4 * PAIR, HALF), BF16),
-            pltpu.VMEM((2, 2 * HALF, 2 * PAIR), BF16),
-            pltpu.VMEM((4, 4 * PATCH, CONTRIB), BF16),
-            pltpu.VMEM((4, 2 * CONTRIB, 2 * PATCH), BF16),
+            pltpu.VMEM((2, 2 * PAIR, 2 * HALF), BF16),
+            pltpu.VMEM((2, HALF, 4 * PAIR), BF16),
+            pltpu.VMEM((4, 2 * PATCH, 2 * CONTRIB), BF16),
+            pltpu.VMEM((4, CONTRIB, 4 * PATCH), BF16),
             pltpu.VMEM((PAIR, 2 * SUBGRID), BF16),
             pltpu.VMEM((2 * SUBGRID, PAIR), BF16),
             pltpu.VMEM((FACETS, SUBGRID), F32),
@@ -593,7 +594,7 @@
             pltpu.VMEM((2, SUBGRID, VIS), F32),
             pltpu.VMEM((2, SUBGRID, SUBGRID), BF16),
             pltpu.VMEM((2, SUBGRID, VIS), BF16),
-            pltpu.VMEM((4, 4 * PATCH, 2 * SUBGRID), BF16),
+            pltpu.VMEM((2, 8 * PATCH, 2 * SUBGRID), BF16),
             chunk,
             chunk,
             chunk,

time: 44.1 us -> 43.7 us (level)
  no operation moved by 1% of the time
where the time goes in v4:
time: 43.7 us; the launch traced here: 43.6 us
  Pallas kernels  42.3 us (97%)
  between operations  1.28 us (3%)
    pallas_call x1, Pallas kernels, on_device(): pl.pallas_call(kernel, out_shape=(jax.ShapeDtypeStruct((ROWS_DEV, PAIR),...  41.2 us
    pallas_call x1, Pallas kernels, on_device(): pl.pallas_call(finish, out_shape=(jax.ShapeDtypeStruct((2 * ROWS_DEV, FAC...  1.12 us

profile of v4, /device:TPU:1, one launch (start us, length us, event | category | flops | bytes accessed | tf_op | source)
XLA Modules:
  0.0 43.6 jit_solution(5957416426148931275)
XLA Ops:
  1.3 41.2 %shard_map.77 = (f32[32,256]{1,0:T(8,128)S(1)}, f32[32,128]{1,0:T(8,128)S(1)}, f32[32,128]{1,0:T(8,128)S(1)}, bf16[256,256]{1,0:T(8,128)(2,1)S(1)}, bf16[16,512]{1,0:T(8,128)(2,1)S(1)}) custom-call(s32[2,16]{1,0:T(2,128)} %bitcast.11, s32[32]{0:T(128)} %starts_in.1, s32[1]{0:T(128)S(6)} %copy.9.col_s, bf16[64,4096]{1,0:T(8,128)(2,1)} %bitcast.8, ...), custom_call_target="tpu_custom_call" | custom-call | tf_op jit(solution)/shard_map/pallas_call | solution.py:564
  42.5 1.1 %shard_map.78 = (bf16[64,4096]{1,0:T(8,128)(2,1)}, bf16[16,512]{1,0:T(8,128)(2,1)}) custom-call(f32[32,256]{1,0:T(8,128)S(1)} %get-tuple-element.9.total, f32[32,128]{1,0:T(8,128)S(1)} %get-tuple-element.10.tw_r, f32[32,128]{1,0:T(8,128)S(1)} %get-tuple-element.11.tw_i, bf16[256,256]{1,0:T(8,128)(2,1)S(1)} %get-tuple-element.12.back_w, ...), custom_call_target="tpu_custom_call" | custom-call | tf_op jit(solution)/shard_map/pallas_call | solution.py:621

commit v5 on v4

--- a/solution.py
+++ b/solution.py
@@ -134,7 +134,6 @@
     eu_r,
     eu_i,
     ev,
-    quad,
     cells,
     weigh,
     shifted,
@@ -432,12 +431,11 @@
         cells[c // 4, low, 0:LANES] = gi.astype(BF16)
         cells[c // 4, low, LANES:] = gr.astype(BF16)
     models_r, models_i = [], []
-    for h in range(2):
-        quad[h] = dot(cells[h], ev[h])
+    inner = [dot(cells[h], ev[h]) for h in range(2)]
     for c in range(SIDE):
         first = PATCH * (c % 4)
-        inner_r = quad[c // 4, first : first + PATCH, :]
-        inner_i = quad[c // 4, LANES + first : LANES + first + PATCH, :]
+        inner_r = inner[c // 4][first : first + PATCH, :]
+        inner_i = inner[c // 4][LANES + first : LANES + first + PATCH, :]
         ur, ui = eu_r[PATCH * c : PATCH * (c + 1), :], eu_i[PATCH * c : PATCH * (c + 1), :]
         models_r.append(jnp.sum(ur * inner_r - ui * inner_i, axis=0, keepdims=True))
         models_i.append(jnp.sum(ur * inner_i + ui * inner_r, axis=0, keepdims=True))
@@ -591,7 +589,6 @@
             pltpu.VMEM((SUBGRID, VIS), F32),
             pltpu.VMEM((SUBGRID, VIS), F32),
             pltpu.VMEM((2, SUBGRID, VIS), BF16),
-            pltpu.VMEM((2, SUBGRID, VIS), F32),
             pltpu.VMEM((2, SUBGRID, SUBGRID), BF16),
             pltpu.VMEM((2, SUBGRID, VIS), BF16),
             pltpu.VMEM((2, 8 * PATCH, 2 * SUBGRID), BF16),

time: 43.7 us -> 43.7 us (level)
  no operation moved by 1% of the time
where the time goes in v5:
time: 43.7 us; the launch traced here: 43.6 us
  Pallas kernels  42.3 us (97%)
  between operations  1.28 us (3%)
    pallas_call x1, Pallas kernels, on_device(): pl.pallas_call(kernel, out_shape=(jax.ShapeDtypeStruct((ROWS_DEV, PAIR),...  41.2 us
    pallas_call x1, Pallas kernels, on_device(): pl.pallas_call(finish, out_shape=(jax.ShapeDtypeStruct((2 * ROWS_DEV, FAC...  1.12 us

profile of v5, /device:TPU:1, one launch (start us, length us, event | category | flops | bytes accessed | tf_op | source)
XLA Modules:
  0.0 43.6 jit_solution(5957416426148931275)
XLA Ops:
  1.3 41.2 %shard_map.77 = (f32[32,256]{1,0:T(8,128)S(1)}, f32[32,128]{1,0:T(8,128)S(1)}, f32[32,128]{1,0:T(8,128)S(1)}, bf16[256,256]{1,0:T(8,128)(2,1)S(1)}, bf16[16,512]{1,0:T(8,128)(2,1)S(1)}) custom-call(s32[2,16]{1,0:T(2,128)} %bitcast.11, s32[32]{0:T(128)} %starts_in.1, s32[1]{0:T(128)S(6)} %copy.9.col_s, bf16[64,4096]{1,0:T(8,128)(2,1)} %bitcast.8, ...), custom_call_target="tpu_custom_call" | custom-call | tf_op jit(solution)/shard_map/pallas_call | solution.py:562
  42.5 1.1 %shard_map.78 = (bf16[64,4096]{1,0:T(8,128)(2,1)}, bf16[16,512]{1,0:T(8,128)(2,1)}) custom-call(f32[32,256]{1,0:T(8,128)S(1)} %get-tuple-element.9.total, f32[32,128]{1,0:T(8,128)S(1)} %get-tuple-element.10.tw_r, f32[32,128]{1,0:T(8,128)S(1)} %get-tuple-element.11.tw_i, bf16[256,256]{1,0:T(8,128)(2,1)S(1)} %get-tuple-element.12.back_w, ...), custom_call_target="tpu_custom_call" | custom-call | tf_op jit(solution)/shard_map/pallas_call | solution.py:618
